TPU v7x, 32 devices: a whole 2x2x4 slice. The times are simulated.
32 devices in a mesh: section: 2 (over core), row: 4 (over y, x), col: 4 (over z).
Axes of the slice: x: 2, y: 2, z: 4, core: 2. Of those that a mesh axis runs over, the one named last changes fastest.
Arguments:
- hidden_in: bfloat16 [2, 2048, 1024], P(None, 'row', 'col'), may hold values from -6 to 6
- cotangent: bfloat16 [2, 2048, 1024], P(None, 'row', 'col'), may hold values from -6 to 6
- lengths: int32 [2, 3], replicated, may hold values from 320 to 1280, as said below
- norm_gains: float32 [2, 2, 1024], P('section', None, 'col'), may hold values from 0.25 to 1.75
- norm_biases: float32 [2, 2, 1024], P('section', None, 'col'), may hold values from -3 to 3
- w_qkv: bfloat16 [2, 3, 1024, 1024], P('section', None, 'row', 'col'), may hold values from -0.1875 to 0.1875
- b_qkv: float32 [2, 3, 1024], P('section', None, 'col'), may hold values from -3 to 3
- w_out: bfloat16 [2, 1024, 1024], P('section', 'col', 'row'), may hold values from -3 to 3
- w_fc: bfloat16 [2, 1024, 4096], P('section', 'row', 'col'), may hold values from -0.1875 to 0.1875
- b_fc: float32 [2, 4096], P('section', 'col'), may hold values from -3 to 3
- w_proj: bfloat16 [2, 4096, 1024], P('section', 'col', 'row'), may hold values from -0.09375 to 0.09375
- b_out: float32 [2, 1024], P('section', 'col'), may hold values from -3 to 3
Outputs:
- layer_out: bfloat16 [2, 2, 2048, 1024], P('section', None, 'row', 'col')
- input_grad: bfloat16 [2, 2, 2048, 1024], P('section', None, 'row', 'col')
- grad_norm_gains: float32 [2, 2, 1024], P('section', None, 'col')
- grad_norm_biases: float32 [2, 2, 1024], P('section', None, 'col')
- grad_w_qkv: float32 [2, 3, 1024, 1024], P('section', None, 'row', 'col')
- grad_b_qkv: float32 [2, 3, 1024], P('section', None, 'col')
- grad_w_out: float32 [2, 1024, 1024], P('section', 'col', 'row')
- grad_w_fc: float32 [2, 1024, 4096], P('section', 'row', 'col')
- grad_b_fc: float32 [2, 4096], P('section', 'col')
- grad_w_proj: float32 [2, 4096, 1024], P('section', 'col', 'row')
- grad_b_out: float32 [2, 1024], P('section', 'col')
Inputs may be any that keep to these rules, and one draw needn't show every extreme that they name: `lengths`: each row sums to 2048; the prompt has between 768 and 1280 tokens, each continuation between 320 and 704.
All inputs are finite; a program needn't handle non-finite values.
Results may differ from a plain program's by a relative error of at most 0.02.
Values may be sent and summed in bfloat16 or wider, within the bound.
A program may use at most 192 MiB of HBM per device.

v0:
```python
from functools import partial
import math

import jax
import jax.numpy as jnp
from jax import lax
from jax.sharding import PartitionSpec as P

MODEL_WIDTH = 1024
HEAD_DIM = 64
ROT = 16


EPS = 1e-05
NEG = -1e30


def from_partner(value, axis, apart):
    mask = 2**apart
    pairs = [(source, source ^ mask) for source in range(lax.axis_size(axis))]
    return lax.ppermute(value, axis, pairs)


def segment_of(token_ids, starts):
    return jnp.sum((token_ids[:, None] >= starts[None, 1:]).astype(jnp.int32), axis=1)


def token_layout(lengths_row, token_ids):
    starts = jnp.cumsum(lengths_row) - lengths_row
    segment = segment_of(token_ids, starts)
    labels = jnp.arange(1, lengths_row.shape[0], dtype=jnp.int32)
    seg_begin = jnp.sum(jnp.where(segment[:, None] == labels[None, :], starts[None, 1:], 0), axis=1)
    position = jnp.where(segment == 0, token_ids, lengths_row[0] + token_ids - seg_begin)
    return (starts, segment, position)


def rotary_tables(position, turned):
    half_rot = turned // 2
    freqs = 10000.0 ** (-(2.0 * jnp.arange(half_rot, dtype=jnp.float32)) / turned)
    angles = position.astype(jnp.float32)[:, None] * freqs[None, :]
    return (jnp.cos(angles), jnp.sin(angles))


def rotate(values, cos_table, sin_table, direction):
    half_rot = cos_table.shape[-1]
    lower = values[..., :half_rot]
    upper = values[..., half_rot : 2 * half_rot]
    cos_cast = cos_table[:, None, :]
    sin_cast = direction * sin_table[:, None, :]
    return jnp.concatenate(
        [
            lower * cos_cast - upper * sin_cast,
            upper * cos_cast + lower * sin_cast,
            values[..., 2 * half_rot :],
        ],
        axis=-1,
    )


def permitted(query_seg, query_tok, key_seg, key_tok):
    from_prompt = (key_seg[None, :] == 0) & (query_seg[:, None] > 0)
    same_causal = (key_seg[None, :] == query_seg[:, None]) & (
        key_tok[None, :] <= query_tok[:, None]
    )
    return from_prompt | same_causal


def attend(running, key_piece, value_piece, query3, layout):
    run_max, run_sum, totals = running
    piece_len = key_piece.shape[0]
    key3 = key_piece.reshape(piece_len, query3.shape[1], query3.shape[2])
    value3 = value_piece.reshape(piece_len, query3.shape[1], query3.shape[2])
    key_tok = jnp.arange(piece_len, dtype=jnp.int32)
    key_seg = segment_of(key_tok, layout["starts"])
    allowed = permitted(layout["segment"], layout["tokens"], key_seg, key_tok)[None]
    scores = jnp.einsum("qhd,khd->hqk", query3, key3, preferred_element_type=jnp.float32) * (
        1.0 / math.sqrt(query3.shape[2])
    )
    masked = jnp.where(allowed, scores, NEG)
    new_max = jnp.maximum(run_max, jnp.max(masked, axis=-1))
    weights = jnp.where(allowed, jnp.exp(masked - new_max[..., None]), 0.0)
    run_sum = jnp.sum(weights, axis=-1)
    totals = jnp.einsum(
        "hqk,khd->hqd", weights.astype(jnp.bfloat16), value3, preferred_element_type=jnp.float32
    )
    return (new_max, run_sum, totals)


def body(
    hidden_in,
    cotangent,
    lengths,
    norm_gains,
    norm_biases,
    w_qkv,
    b_qkv,
    w_out,
    w_fc,
    b_fc,
    w_proj,
    b_out,
):
    micro_count = hidden_in.shape[0]
    row_tokens = hidden_in.shape[1]
    local_width = hidden_in.shape[2]
    total_tokens = row_tokens * lax.axis_size("row")
    heads_local = local_width // HEAD_DIM
    score_scale = 1.0 / math.sqrt(HEAD_DIM)
    key_block = min(512, total_tokens)
    is_first = lax.axis_index("section") == 0
    my_tokens = lax.axis_index("row") * row_tokens + jnp.arange(row_tokens, dtype=jnp.int32)
    complete_gains, complete_shifts = (
        lax.all_gather(norm_gains[0], "col", axis=1, tiled=True),
        lax.all_gather(norm_biases[0], "col", axis=1, tiled=True),
    )
    w_query, w_output, w_hidden, w_project = (
        lax.all_gather(w_qkv[0], "row", axis=1, tiled=True),
        lax.all_gather(w_out[0], "row", axis=1, tiled=True),
        lax.all_gather(w_fc[0], "row", axis=0, tiled=True),
        lax.all_gather(w_proj[0], "row", axis=1, tiled=True),
    )
    b_query = b_qkv[0]
    b_hidden = b_fc[0]
    b_output = b_out[0]
    resident_gains = norm_gains[0]
    shaped = (row_tokens, heads_local, HEAD_DIM)
    zero_rows = jnp.zeros((row_tokens, local_width), jnp.bfloat16)
    received = zero_rows
    large_acc = (
        jnp.zeros(w_query.shape, jnp.float32),
        jnp.zeros(w_output.shape, jnp.float32),
        jnp.zeros(w_hidden.shape, jnp.float32),
        jnp.zeros(w_project.shape, jnp.float32),
    )
    small_acc = (
        jnp.zeros((2, local_width), jnp.float32),
        jnp.zeros((2, local_width), jnp.float32),
        jnp.zeros((3, local_width), jnp.float32),
        jnp.zeros(b_hidden.shape, jnp.float32),
        jnp.zeros((local_width,), jnp.float32),
    )
    states = []
    forward_outs = []
    backward_outs = []
    for moment in range(micro_count + 2):
        first_index = min(moment, micro_count - 1)
        second_index = min(max(moment - 1, 0), micro_count - 1)
        starts, segment, position = token_layout(
            jnp.where(is_first, lengths[first_index], lengths[second_index]), my_tokens
        )
        cos_table, sin_table = rotary_tables(position, ROT)
        layout = {
            "starts": starts,
            "segment": segment,
            "tokens": my_tokens,
            "cos_table": cos_table,
            "sin_table": sin_table,
        }
        first_input = hidden_in[moment] if moment < micro_count else zero_rows
        layer_entry_input = jnp.where(is_first, first_input, received)
        gathered = lax.all_gather(layer_entry_input, "col", axis=1, tiled=True)
        as_float = gathered.astype(jnp.float32)
        row_average_value = jnp.mean(as_float, axis=1, keepdims=True)
        centred_rows = as_float - row_average_value
        row_inverse_spread = lax.rsqrt(
            jnp.mean(centred_rows * centred_rows, axis=1, keepdims=True) + EPS
        )
        complete_unit_rows = centred_rows * row_inverse_spread
        attention_normed_rows = (
            complete_unit_rows * complete_gains[0] + complete_shifts[0]
        ).astype(jnp.bfloat16)
        feedforward_normed_rows = (
            complete_unit_rows * complete_gains[1] + complete_shifts[1]
        ).astype(jnp.bfloat16)
        projected = (
            jnp.einsum(
                "td,cde->cte", attention_normed_rows, w_query, preferred_element_type=jnp.float32
            )
            + b_query[:, None, :]
        )
        forward_query3 = rotate(
            projected[0].reshape(shaped), layout["cos_table"], layout["sin_table"], 1.0
        ).astype(jnp.bfloat16)
        key_flat = (
            rotate(projected[1].reshape(shaped), layout["cos_table"], layout["sin_table"], 1.0)
            .reshape(row_tokens, local_width)
            .astype(jnp.bfloat16)
        )
        value_flat = projected[2].astype(jnp.bfloat16)
        initial = (
            jnp.full((heads_local, row_tokens), NEG, jnp.float32),
            jnp.zeros((heads_local, row_tokens), jnp.float32),
            jnp.zeros((heads_local, row_tokens, HEAD_DIM), jnp.float32),
        )
        kept_state = {}
        running = attend(
            initial,
            lax.all_gather(key_flat, "row", axis=0, tiled=True),
            lax.all_gather(value_flat, "row", axis=0, tiled=True),
            forward_query3,
            layout,
        )
        run_max, run_sum, totals = running
        out_exact = totals / run_sum[..., None]
        log_sum = run_max + jnp.log(run_sum)
        attn_flat = (
            jnp.transpose(out_exact, (1, 0, 2))
            .reshape(row_tokens, local_width)
            .astype(jnp.bfloat16)
        )
        hidden_pre = (
            jnp.dot(feedforward_normed_rows, w_hidden, preferred_element_type=jnp.float32)
            + b_hidden
        )
        hidden = jax.nn.gelu(hidden_pre, approximate=False).astype(jnp.bfloat16)
        branch_terms = jnp.dot(attn_flat, w_output, preferred_element_type=jnp.float32) + jnp.dot(
            hidden, w_project, preferred_element_type=jnp.float32
        )
        summed = lax.psum_scatter(
            branch_terms.astype(jnp.bfloat16), "col", scatter_dimension=1, tiled=True
        ).astype(jnp.float32)
        output = (layer_entry_input.astype(jnp.float32) + summed + b_output).astype(jnp.bfloat16)
        kept_state["layer_input"] = layer_entry_input
        kept_state["gathered"] = gathered
        kept_state["row_mean"] = row_average_value
        kept_state["row_rstd"] = row_inverse_spread
        kept_state["normed_a"] = attention_normed_rows
        kept_state["normed_m"] = feedforward_normed_rows
        kept_state["query3"] = forward_query3
        kept_state["key_flat"] = key_flat
        kept_state["value_flat"] = value_flat
        kept_state["attn_flat"] = attn_flat
        kept_state["out_exact"] = out_exact
        kept_state["log_sum"] = log_sum
        kept_state["hidden_pre"] = hidden_pre
        kept_state["hidden"] = hidden
        kept_state["starts"] = layout["starts"]
        kept_state["segment"] = layout["segment"]
        kept_state["cos_table"] = layout["cos_table"]
        kept_state["sin_table"] = layout["sin_table"]
        output, current = (output, kept_state)
        states.append(current)
        earlier_state = states[moment - 2] if moment >= 2 else current
        stored_values = jax.tree.map(
            lambda earlier, latest: jnp.where(is_first, earlier, latest), earlier_state, current
        )
        cot_now = cotangent[moment - 1] if 1 <= moment <= micro_count else zero_rows
        grad_in = jnp.where(is_first, received, cot_now)
        grad_full = lax.all_gather(grad_in, "col", axis=1, tiled=True)
        grad_wout = jnp.einsum(
            "te,td->ed", stored_values["attn_flat"], grad_full, preferred_element_type=jnp.float32
        )
        grad_wproj = jnp.einsum(
            "tf,td->fd", stored_values["hidden"], grad_full, preferred_element_type=jnp.float32
        )
        grad_bout = jnp.sum(grad_in.astype(jnp.float32), axis=0)
        grad_attn = jnp.einsum(
            "td,ed->te", grad_full, w_output, preferred_element_type=jnp.float32
        ).astype(jnp.bfloat16)
        grad_hidden = jnp.einsum(
            "td,fd->tf", grad_full, w_project, preferred_element_type=jnp.float32
        )
        gelu_value, gelu_back = jax.vjp(
            partial(jax.nn.gelu, approximate=False), stored_values["hidden_pre"]
        )
        grad_hpre = gelu_back(grad_hidden)[0].astype(jnp.bfloat16)
        grad_wfc = jnp.einsum(
            "td,tf->df", stored_values["normed_m"], grad_hpre, preferred_element_type=jnp.float32
        )
        grad_bfc = jnp.sum(grad_hpre.astype(jnp.float32), axis=0)
        grad_normed_m = jnp.einsum(
            "tf,df->td", grad_hpre, w_hidden, preferred_element_type=jnp.float32
        )
        key_full = lax.all_gather(stored_values["key_flat"], "row", axis=0, tiled=True)
        value_full = lax.all_gather(stored_values["value_flat"], "row", axis=0, tiled=True)
        grad_out3 = grad_attn.reshape(shaped)
        query3 = stored_values["query3"]
        delta = jnp.sum(
            jnp.transpose(grad_out3.astype(jnp.float32), (1, 0, 2)) * stored_values["out_exact"],
            axis=-1,
        )
        grad_query = jnp.zeros(shaped, jnp.float32)
        key_terms = []
        value_terms = []
        for block_no in range(total_tokens // key_block):
            begin_at = block_no * key_block
            key_part = key_full[begin_at : begin_at + key_block].reshape(
                key_block, heads_local, HEAD_DIM
            )
            value_part = value_full[begin_at : begin_at + key_block].reshape(
                key_block, heads_local, HEAD_DIM
            )
            key_tok = begin_at + jnp.arange(key_block, dtype=jnp.int32)
            key_seg = segment_of(key_tok, stored_values["starts"])
            allowed = permitted(stored_values["segment"], my_tokens, key_seg, key_tok)[None]
            scores = (
                jnp.einsum("qhd,khd->hqk", query3, key_part, preferred_element_type=jnp.float32)
                * score_scale
            )
            probs = jnp.where(
                allowed,
                jnp.exp(jnp.where(allowed, scores, NEG) - stored_values["log_sum"][..., None]),
                0.0,
            )
            grad_probs = jnp.einsum(
                "qhd,khd->hqk", grad_out3, value_part, preferred_element_type=jnp.float32
            )
            grad_scores = (probs * (grad_probs - delta[..., None])).astype(jnp.bfloat16)
            grad_query = grad_query + jnp.einsum(
                "hqk,khd->qhd", grad_scores, key_part, preferred_element_type=jnp.float32
            )
            key_terms.append(
                jnp.einsum(
                    "hqk,qhd->khd", grad_scores, query3, preferred_element_type=jnp.float32
                ).reshape(key_block, local_width)
                * score_scale
            )
            value_terms.append(
                jnp.einsum(
                    "hqk,qhd->khd",
                    probs.astype(jnp.bfloat16),
                    grad_out3,
                    preferred_element_type=jnp.float32,
                ).reshape(key_block, local_width)
            )
        grad_query = grad_query * score_scale
        kv_terms = jnp.concatenate(
            [jnp.concatenate(key_terms, axis=0), jnp.concatenate(value_terms, axis=0)], axis=1
        )
        kv_grads = lax.psum_scatter(
            kv_terms.astype(jnp.bfloat16), "row", scatter_dimension=0, tiled=True
        ).astype(jnp.float32)
        grad_key = kv_grads[:, :local_width].reshape(shaped)
        grad_value = kv_grads[:, local_width:]
        grad_pre = jnp.stack(
            [
                rotate(
                    grad_query, stored_values["cos_table"], stored_values["sin_table"], -1.0
                ).reshape(row_tokens, local_width),
                rotate(
                    grad_key, stored_values["cos_table"], stored_values["sin_table"], -1.0
                ).reshape(row_tokens, local_width),
                grad_value,
            ]
        ).astype(jnp.bfloat16)
        grad_wqkv = jnp.einsum(
            "td,cte->cde", stored_values["normed_a"], grad_pre, preferred_element_type=jnp.float32
        )
        grad_bqkv = jnp.sum(grad_pre.astype(jnp.float32), axis=1)
        grad_normed_a = jnp.einsum(
            "cte,cde->td", grad_pre, w_query, preferred_element_type=jnp.float32
        )
        resident_unit_rows = (
            stored_values["layer_input"].astype(jnp.float32) - stored_values["row_mean"]
        ) * stored_values["row_rstd"]
        attention_norm_portion = lax.psum_scatter(
            grad_normed_a.astype(jnp.bfloat16), "col", scatter_dimension=1, tiled=True
        ).astype(jnp.float32)
        feedforward_norm_portion = lax.psum_scatter(
            grad_normed_m.astype(jnp.bfloat16), "col", scatter_dimension=1, tiled=True
        ).astype(jnp.float32)
        gradient_unit_rows = (
            attention_norm_portion * resident_gains[0]
            + feedforward_norm_portion * resident_gains[1]
        )
        grad_gains = jnp.stack(
            [
                jnp.sum(attention_norm_portion * resident_unit_rows, axis=0),
                jnp.sum(feedforward_norm_portion * resident_unit_rows, axis=0),
            ]
        )
        grad_shifts = jnp.stack(
            [jnp.sum(attention_norm_portion, axis=0), jnp.sum(feedforward_norm_portion, axis=0)]
        )
        row_sum_totals = lax.psum(
            jnp.stack(
                [
                    jnp.sum(gradient_unit_rows, axis=1),
                    jnp.sum(gradient_unit_rows * resident_unit_rows, axis=1),
                ]
            ),
            "col",
        )
        grad_input = grad_in.astype(jnp.float32) + stored_values["row_rstd"] * (
            gradient_unit_rows
            - row_sum_totals[0][:, None] / MODEL_WIDTH
            - resident_unit_rows * row_sum_totals[1][:, None] / MODEL_WIDTH
        )
        large_part = (grad_wqkv, grad_wout, grad_wfc, grad_wproj)
        small_part = (grad_gains, grad_shifts, grad_bqkv, grad_bfc, grad_bout)
        grad_input, large_part, small_part = (
            grad_input.astype(jnp.bfloat16),
            large_part,
            small_part,
        )
        live_mask = jnp.where(
            is_first, 1.0 if moment >= 2 else 0.0, 1.0 if 1 <= moment <= micro_count else 0.0
        ).astype(jnp.float32)
        large_masked = tuple((member * live_mask for member in large_part))
        small_acc = tuple(
            (total + member * live_mask for total, member in zip(small_acc, small_part))
        )
        large_acc = tuple((total + member for total, member in zip(large_acc, large_masked)))
        forward_outs.append(output)
        backward_outs.append(grad_input)
        if moment < micro_count + 1:
            received = from_partner(jnp.where(is_first, output, grad_input), "section", 0)
    out_rows = jnp.stack(
        [
            jnp.where(is_first, forward_outs[batch_no], forward_outs[batch_no + 1])
            for batch_no in range(micro_count)
        ]
    )[None]
    grad_rows_out = jnp.stack(
        [
            jnp.where(is_first, backward_outs[batch_no + 2], backward_outs[batch_no + 1])
            for batch_no in range(micro_count)
        ]
    )[None]
    large_shards = (
        lax.psum_scatter(
            large_acc[0].astype(jnp.bfloat16), "row", scatter_dimension=1, tiled=True
        ).astype(jnp.float32),
        lax.psum_scatter(
            large_acc[1].astype(jnp.bfloat16), "row", scatter_dimension=1, tiled=True
        ).astype(jnp.float32),
        lax.psum_scatter(
            large_acc[2].astype(jnp.bfloat16), "row", scatter_dimension=0, tiled=True
        ).astype(jnp.float32),
        lax.psum_scatter(
            large_acc[3].astype(jnp.bfloat16), "row", scatter_dimension=1, tiled=True
        ).astype(jnp.float32),
    )
    small_sums = lax.psum(small_acc, "row")
    return (
        out_rows,
        grad_rows_out,
        small_sums[0][None],
        small_sums[1][None],
        large_shards[0][None],
        small_sums[2][None],
        large_shards[1][None],
        large_shards[2][None],
        small_sums[3][None],
        large_shards[3][None],
        small_sums[4][None],
    )


def solution(mesh):
    return jax.shard_map(
        body,
        mesh=mesh,
        in_specs=(
            P(None, "row", "col"),
            P(None, "row", "col"),
            P(),
            P("section", None, "col"),
            P("section", None, "col"),
            P("section", None, "row", "col"),
            P("section", None, "col"),
            P("section", "col", "row"),
            P("section", "row", "col"),
            P("section", "col"),
            P("section", "col", "row"),
            P("section", "col"),
        ),
        out_specs=(
            P("section", None, "row", "col"),
            P("section", None, "row", "col"),
            P("section", None, "col"),
            P("section", None, "col"),
            P("section", None, "row", "col"),
            P("section", None, "col"),
            P("section", "col", "row"),
            P("section", "row", "col"),
            P("section", "col"),
            P("section", "col", "row"),
            P("section", "col"),
        ),
        check_vma=False,
    )
```

profile of v0, /device:TPU:0, one launch (start us, length us, event | category | flops | bytes accessed | tf_op | source)
XLA Modules:
  0.0 1431.4 jit_solution(9654369469626075461)
XLA Ops:
  12.1 13.6 all-gather.1
  46.2 27.6 %all-gather.62.cloned.1.call-done = bf16[1,3,1024,256]{2,3,1,0:T(8,128)(2,1)} async-done(((bf16[1,3,256,256]{2,3,1,0:T(8,128)(2,1)}), bf16[1,3,1024,256]{2,3,1,0:T(8,128)(2,1)}) %all-gather.62.cloned.1.call-update) | async-done | bytes 1572880 | tf_op jit(solution)/shard_map/all_gather | solution.py:117
  82.2 14.7 %all-gather.5 = bf16[1,256,1024]{2,1,0:T(8,128)(2,1)S(1)} all-gather(bf16[1,256,256]{2,1,0:T(8,128)(2,1)S(1)} %copy-done.182), channel_id=7, replica_groups=mesh['section'=2,'row'=4,'col'=4] {'row'}, dimensions={2}, use_global_device_ids=true | all-gather | bytes 655360 | tf_op jit(solution)/shard_map/all_gather | solution.py:118
  230.6 17.2 %reduce-scatter.22.cloned.1.call-done = bf16[512,512]{1,0:T(8,128)(2,1)} async-done(((bf16[2048,512]{1,0:T(8,128)(2,1)}), bf16[512,512]{1,0:T(8,128)(2,1)}) %reduce-scatter.22.cloned.1.call-update) | async-done | bytes 524304 | tf_op jit(solution)/shard_map/reduce_scatter | solution.py:330
  259.6 17.8 %reduce-scatter.26.cloned.1.call-done = bf16[512,256]{0,1:T(8,128)(2,1)} async-done(((bf16[512,1024]{0,1:T(8,128)(2,1)}), bf16[512,256]{0,1:T(8,128)(2,1)}) %reduce-scatter.26.cloned.1.call-update) | async-done | bytes 262160 | tf_op jit(solution)/shard_map/reduce_scatter | solution.py:359
  277.4 28.1 %reduce-scatter.24.cloned.1.call-done = bf16[512,256]{0,1:T(8,128)(2,1)} async-done(((bf16[512,1024]{0,1:T(8,128)(2,1)}), bf16[512,256]{0,1:T(8,128)(2,1)}) %reduce-scatter.24.cloned.1.call-update) | async-done | bytes 262160 | tf_op jit(solution)/shard_map/reduce_scatter | solution.py:356
  317.1 16.6 %reduce-scatter.20.cloned.1.call-done = bf16[512,256]{0,1:T(8,128)(2,1)} async-done(((bf16[512,1024]{0,1:T(8,128)(2,1)}), bf16[512,256]{0,1:T(8,128)(2,1)}) %reduce-scatter.20.cloned.1.call-update) | async-done | bytes 262160 | tf_op jit(solution)/shard_map/reduce_scatter | solution.py:219
  339.9 24.3 %all-gather.38.cloned.1.call-done = bf16[512,1024]{0,1:T(8,128)(2,1)} async-done(((bf16[512,256]{0,1:T(8,128)(2,1)}), bf16[512,1024]{0,1:T(8,128)(2,1)}) %all-gather.38.cloned.1.call-update) | async-done | bytes 1048592 | tf_op jit(solution)/shard_map/all_gather | solution.py:161
  378.0 15.1 %all-gather.42.cloned.1.call-done = bf16[512,1024]{0,1:T(8,128)(2,1)} async-done(((bf16[512,256]{0,1:T(8,128)(2,1)}), bf16[512,1024]{0,1:T(8,128)(2,1)}) %all-gather.42.cloned.1.call-update) | async-done | bytes 1048592 | tf_op jit(solution)/shard_map/all_gather | solution.py:249
  395.4 26.1 %all-gather.40.cloned.1.call-done = bf16[2048,256]{0,1:T(8,128)(2,1)} async-done(((bf16[512,256]{0,1:T(8,128)(2,1)}), bf16[2048,256]{0,1:T(8,128)(2,1)}) %all-gather.40.cloned.1.call-update) | async-done | bytes 1048592 | tf_op jit(solution)/shard_map/all_gather | solution.py:198
  543.3 24.1 %reduce-scatter.28.cloned.1.call-done = bf16[512,256]{0,1:T(8,128)(2,1)} async-done(((bf16[512,1024]{0,1:T(8,128)(2,1)}), bf16[512,256]{0,1:T(8,128)(2,1)}) %reduce-scatter.28.cloned.1.call-update) | async-done | bytes 262160 | tf_op jit(solution)/shard_map/reduce_scatter | solution.py:219
  569.2 26.1 %reduce-scatter.34.cloned.1.call-done = bf16[512,256]{0,1:T(8,128)(2,1)} async-done(((bf16[512,1024]{0,1:T(8,128)(2,1)}), bf16[512,256]{0,1:T(8,128)(2,1)}) %reduce-scatter.34.cloned.1.call-update) | async-done | bytes 262160 | tf_op jit(solution)/shard_map/reduce_scatter | solution.py:359
  595.3 28.1 %reduce-scatter.32.cloned.1.call-done = bf16[512,256]{0,1:T(8,128)(2,1)} async-done(((bf16[512,1024]{0,1:T(8,128)(2,1)}), bf16[512,256]{0,1:T(8,128)(2,1)}) %reduce-scatter.32.cloned.1.call-update) | async-done | bytes 262160 | tf_op jit(solution)/shard_map/reduce_scatter | solution.py:356
  641.1 25.0 %all-gather.44.cloned.1.call-done = bf16[512,1024]{0,1:T(8,128)(2,1)} async-done(((bf16[512,256]{0,1:T(8,128)(2,1)}), bf16[512,1024]{0,1:T(8,128)(2,1)}) %all-gather.44.cloned.1.call-update) | async-done | bytes 1048592 | tf_op jit(solution)/shard_map/all_gather | solution.py:161
  682.5 12.4 all-gather.50.cloned.1.call-done
  697.3 26.1 %all-gather.46.cloned.1.call-done = bf16[2048,256]{0,1:T(8,128)(2,1)} async-done(((bf16[512,256]{0,1:T(8,128)(2,1)}), bf16[2048,256]{0,1:T(8,128)(2,1)}) %all-gather.46.cloned.1.call-update) | async-done | bytes 1048592 | tf_op jit(solution)/shard_map/all_gather | solution.py:198
  733.7 18.0 %all-gather.48.cloned.1.call-done = bf16[2048,256]{0,1:T(8,128)(2,1)} async-done(((bf16[512,256]{0,1:T(8,128)(2,1)}), bf16[2048,256]{0,1:T(8,128)(2,1)}) %all-gather.48.cloned.1.call-update) | async-done | bytes 1048592 | tf_op jit(solution)/shard_map/all_gather | solution.py:274
  759.3 20.8 %all-gather.72.cloned.1.call-done = bf16[1,2048,256]{1,2,0:T(8,128)(2,1)} async-done(((bf16[1,512,256]{1,2,0:T(8,128)(2,1)}), bf16[1,2048,256]{1,2,0:T(8,128)(2,1)}) %all-gather.72.cloned.1.call-update) | async-done | bytes 1048592 | tf_op jit(solution)/shard_map/all_gather | solution.py:199
  789.1 19.2 %all-gather.76.cloned.1.call-done = bf16[1,2048,256]{1,2,0:T(8,128)(2,1)} async-done(((bf16[1,512,256]{1,2,0:T(8,128)(2,1)}), bf16[1,2048,256]{1,2,0:T(8,128)(2,1)}) %all-gather.76.cloned.1.call-update) | async-done | bytes 1048592 | tf_op jit(solution)/shard_map/all_gather | solution.py:275
  917.2 28.5 %reduce-scatter.40.cloned.1.call-done = bf16[512,256]{0,1:T(8,128)(2,1)} async-done(((bf16[512,1024]{0,1:T(8,128)(2,1)}), bf16[512,256]{0,1:T(8,128)(2,1)}) %reduce-scatter.40.cloned.1.call-update) | async-done | bytes 262160 | tf_op jit(solution)/shard_map/reduce_scatter | solution.py:356
  960.2 13.8 reduce-scatter.36.cloned.1.call-done
  979.8 25.3 %all-gather.52.cloned.1.call-done = bf16[512,1024]{0,1:T(8,128)(2,1)} async-done(((bf16[512,256]{0,1:T(8,128)(2,1)}), bf16[512,1024]{0,1:T(8,128)(2,1)}) %all-gather.52.cloned.1.call-update) | async-done | bytes 1048592 | tf_op jit(solution)/shard_map/all_gather | solution.py:161
  1021.8 12.1 all-gather.58.cloned.1.call-done
  1036.3 26.1 %all-gather.56.cloned.1.call-done = bf16[2048,256]{0,1:T(8,128)(2,1)} async-done(((bf16[512,256]{0,1:T(8,128)(2,1)}), bf16[2048,256]{0,1:T(8,128)(2,1)}) %all-gather.56.cloned.1.call-update) | async-done | bytes 1048592 | tf_op jit(solution)/shard_map/all_gather | solution.py:198
  1072.7 18.1 %all-gather.54.cloned.1.call-done = bf16[2048,256]{0,1:T(8,128)(2,1)} async-done(((bf16[512,256]{0,1:T(8,128)(2,1)}), bf16[2048,256]{0,1:T(8,128)(2,1)}) %all-gather.54.cloned.1.call-update) | async-done | bytes 1048592 | tf_op jit(solution)/shard_map/all_gather | solution.py:274
  1098.3 20.6 %all-gather.74.cloned.1.call-done = bf16[1,2048,256]{1,2,0:T(8,128)(2,1)} async-done(((bf16[1,512,256]{1,2,0:T(8,128)(2,1)}), bf16[1,2048,256]{1,2,0:T(8,128)(2,1)}) %all-gather.74.cloned.1.call-update) | async-done | bytes 1048592 | tf_op jit(solution)/shard_map/all_gather | solution.py:199
  1128.0 19.3 %all-gather.78.cloned.1.call-done = bf16[1,2048,256]{1,2,0:T(8,128)(2,1)} async-done(((bf16[1,512,256]{1,2,0:T(8,128)(2,1)}), bf16[1,2048,256]{1,2,0:T(8,128)(2,1)}) %all-gather.78.cloned.1.call-update) | async-done | bytes 1048592 | tf_op jit(solution)/shard_map/all_gather | solution.py:275
  1274.0 19.3 %reduce-scatter.56.cloned.1.call-done = bf16[1024,256]{1,0:T(8,128)(2,1)} async-done(((bf16[1024,1024]{1,0:T(8,128)(2,1)}), bf16[1024,256]{1,0:T(8,128)(2,1)}) %reduce-scatter.56.cloned.1.call-update) | async-done | bytes 524304 | tf_op jit(solution)/shard_map/reduce_scatter | solution.py:430
  1295.4 36.4 %reduce-scatter.54.cloned.1.call-done = bf16[256,1024]{1,0:T(8,128)(2,1)} async-done(((bf16[1024,1024]{1,0:T(8,128)(2,1)}), bf16[256,1024]{1,0:T(8,128)(2,1)}) %reduce-scatter.54.cloned.1.call-update) | async-done | bytes 524304 | tf_op jit(solution)/shard_map/reduce_scatter | solution.py:427
  1334.1 27.0 %reduce-scatter.48.cloned.1.call-done = bf16[512,256]{0,1:T(8,128)(2,1)} async-done(((bf16[512,1024]{0,1:T(8,128)(2,1)}), bf16[512,256]{0,1:T(8,128)(2,1)}) %reduce-scatter.48.cloned.1.call-update) | async-done | bytes 262160 | tf_op jit(solution)/shard_map/reduce_scatter | solution.py:359
  1361.1 28.2 %reduce-scatter.46.cloned.1.call-done = bf16[512,256]{0,1:T(8,128)(2,1)} async-done(((bf16[512,1024]{0,1:T(8,128)(2,1)}), bf16[512,256]{0,1:T(8,128)(2,1)}) %reduce-scatter.46.cloned.1.call-update) | async-done | bytes 262160 | tf_op jit(solution)/shard_map/reduce_scatter | solution.py:356
  1403.1 16.7 %all-reduce = (f32[1,2,256]{2,1,0:T(2,128)}, f32[1,2,256]{2,1,0:T(2,128)}, f32[1,3,256]{2,0,1:T(1,128)}, f32[1,1024]{1,0:T(1,128)}, f32[1,256]{1,0:T(1,128)}) all-reduce(f32[1,2,256]{2,1,0:T(2,128)S(1)} %fusion.511, f32[1,2,256]{2,1,0:T(2,128)S(1)} %fusion.510, ...), channel_id=1, replica_groups=mesh['section'=2,'row'=4,'col'=4] {'row'}, use_global_device_ids=true, to_apply=%region_83.84 | all-reduce | flops 3072 | bytes 24576 | tf_op jit(solution)/shard_map/psum | solution.py:434
  (1120 shorter events, 720.2 us)
Async XLA Ops:
  11.0 96.7 %all-gather.36.cloned.1.call-start = ((), (), s32[]{:S(2)}) async-start(), calls=%async_computation.19 | async-start | bytes 1310720 | tf_op jit(solution)/shard_map/all_gather | solution.py:198
  80.1 124.8 %all-gather.66.cloned.1.call-start = ((), (), s32[]{:S(2)}) async-start(), calls=%async_computation.53 | async-start | bytes 2621440 | tf_op jit(solution)/shard_map/all_gather | solution.py:119
  80.7 134.7 %all-gather.68.cloned.1.call-start = ((), (), s32[]{:S(2)}) async-start(), calls=%async_computation.54 | async-start | bytes 2621440 | tf_op jit(solution)/shard_map/all_gather | solution.py:120
  81.3 166.5 %reduce-scatter.22.cloned.1.call-start = ((), (), s32[]{:S(2)}) async-start(), calls=%async_computation.21 | async-start | bytes 2621440 | tf_op jit(solution)/shard_map/reduce_scatter | solution.py:330
  224.3 81.3 %reduce-scatter.24.cloned.1.call-start = ((), (), s32[]{:S(2)}) async-start(), calls=%async_computation.22 | async-start | bytes 1310720 | tf_op jit(solution)/shard_map/reduce_scatter | solution.py:356
  254.8 78.8 %reduce-scatter.20.cloned.1.call-start = ((), (), s32[]{:S(2)}) async-start(), calls=%async_computation.20 | async-start | bytes 1310720 | tf_op jit(solution)/shard_map/reduce_scatter | solution.py:219
  259.5 104.7 %all-gather.38.cloned.1.call-start = ((), (), s32[]{:S(2)}) async-start(), calls=%async_computation.24 | async-start | bytes 1310720 | tf_op jit(solution)/shard_map/all_gather | solution.py:161
  339.8 81.6 %all-gather.40.cloned.1.call-start = ((), (), s32[]{:S(2)}) async-start(), calls=%async_computation.25 | async-start | bytes 1310720 | tf_op jit(solution)/shard_map/all_gather | solution.py:198
  372.4 77.9 %all-gather.70.cloned.1.call-start = ((), (), s32[]{:S(2)}) async-start(), calls=%async_computation.55 | async-start | bytes 1310720 | tf_op jit(solution)/shard_map/all_gather | solution.py:199
  377.9 160.0 %reduce-scatter.30.cloned.1.call-start = ((), (), s32[]{:S(2)}) async-start(), calls=%async_computation.28 | async-start | bytes 2621440 | tf_op jit(solution)/shard_map/reduce_scatter | solution.py:330
  515.6 79.7 %reduce-scatter.34.cloned.1.call-start = ((), (), s32[]{:S(2)}) async-start(), calls=%async_computation.30 | async-start | bytes 1310720 | tf_op jit(solution)/shard_map/reduce_scatter | solution.py:359
  524.7 98.7 %reduce-scatter.32.cloned.1.call-start = ((), (), s32[]{:S(2)}) async-start(), calls=%async_computation.29 | async-start | bytes 1310720 | tf_op jit(solution)/shard_map/reduce_scatter | solution.py:356
  543.2 122.9 %all-gather.44.cloned.1.call-start = ((), (), s32[]{:S(2)}) async-start(), calls=%async_computation.31 | async-start | bytes 1310720 | tf_op jit(solution)/shard_map/all_gather | solution.py:161
  641.0 82.4 %all-gather.46.cloned.1.call-start = ((), (), s32[]{:S(2)}) async-start(), calls=%async_computation.32 | async-start | bytes 1310720 | tf_op jit(solution)/shard_map/all_gather | solution.py:198
  675.1 76.7 %all-gather.48.cloned.1.call-start = ((), (), s32[]{:S(2)}) async-start(), calls=%async_computation.34 | async-start | bytes 1310720 | tf_op jit(solution)/shard_map/all_gather | solution.py:274
  676.8 103.3 %all-gather.72.cloned.1.call-start = ((), (), s32[]{:S(2)}) async-start(), calls=%async_computation.56 | async-start | bytes 1310720 | tf_op jit(solution)/shard_map/all_gather | solution.py:199
  678.9 129.3 %all-gather.76.cloned.1.call-start = ((), (), s32[]{:S(2)}) async-start(), calls=%async_computation.58 | async-start | bytes 1310720 | tf_op jit(solution)/shard_map/all_gather | solution.py:275
  682.4 205.3 %reduce-scatter.38.cloned.1.call-start = ((), (), s32[]{:S(2)}) async-start(), calls=%async_computation.36 | async-start | bytes 2621440 | tf_op jit(solution)/shard_map/reduce_scatter | solution.py:330
  872.7 73.0 %reduce-scatter.40.cloned.1.call-start = ((), (), s32[]{:S(2)}) async-start(), calls=%async_computation.37 | async-start | bytes 1310720 | tf_op jit(solution)/shard_map/reduce_scatter | solution.py:356
  901.1 72.9 %reduce-scatter.36.cloned.1.call-start = ((), (), s32[]{:S(2)}) async-start(), calls=%async_computation.33 | async-start | bytes 1310720 | tf_op jit(solution)/shard_map/reduce_scatter | solution.py:219
  907.0 98.1 %all-gather.52.cloned.1.call-start = ((), (), s32[]{:S(2)}) async-start(), calls=%async_computation.39 | async-start | bytes 1310720 | tf_op jit(solution)/shard_map/all_gather | solution.py:161
  979.7 82.6 %all-gather.56.cloned.1.call-start = ((), (), s32[]{:S(2)}) async-start(), calls=%async_computation.41 | async-start | bytes 1310720 | tf_op jit(solution)/shard_map/all_gather | solution.py:198
  1014.0 76.7 %all-gather.54.cloned.1.call-start = ((), (), s32[]{:S(2)}) async-start(), calls=%async_computation.40 | async-start | bytes 1310720 | tf_op jit(solution)/shard_map/all_gather | solution.py:274
  1015.8 103.1 %all-gather.74.cloned.1.call-start = ((), (), s32[]{:S(2)}) async-start(), calls=%async_computation.57 | async-start | bytes 1310720 | tf_op jit(solution)/shard_map/all_gather | solution.py:199
  1017.9 129.4 %all-gather.78.cloned.1.call-start = ((), (), s32[]{:S(2)}) async-start(), calls=%async_computation.59 | async-start | bytes 1310720 | tf_op jit(solution)/shard_map/all_gather | solution.py:275
  1021.6 231.5 %reduce-scatter.44.cloned.1.call-start = ((), (), s32[]{:S(2)}) async-start(), calls=%async_computation.43 | async-start | bytes 2621440 | tf_op jit(solution)/shard_map/reduce_scatter | solution.py:330
  1191.6 80.7 %reduce-scatter.52.cloned.1.call-start = ((), (), s32[]{:S(2)}) async-start(), calls=%async_computation.47 | async-start | bytes 655360 | tf_op jit(solution)/shard_map/reduce_scatter | solution.py:424
  1210.6 82.7 %reduce-scatter.56.cloned.1.call-start = ((), (), s32[]{:S(2)}) async-start(), calls=%async_computation.49 | async-start | bytes 2621440 | tf_op jit(solution)/shard_map/reduce_scatter | solution.py:430
  1221.7 110.1 %reduce-scatter.54.cloned.1.call-start = ((), (), s32[]{:S(2)}) async-start(), calls=%async_computation.48 | async-start | bytes 2621440 | tf_op jit(solution)/shard_map/reduce_scatter | solution.py:427
  1241.5 119.6 %reduce-scatter.48.cloned.1.call-start = ((), (), s32[]{:S(2)}) async-start(), calls=%async_computation.45 | async-start | bytes 1310720 | tf_op jit(solution)/shard_map/reduce_scatter | solution.py:359
  1245.7 143.6 %reduce-scatter.46.cloned.1.call-start = ((), (), s32[]{:S(2)}) async-start(), calls=%async_computation.44 | async-start | bytes 1310720 | tf_op jit(solution)/shard_map/reduce_scatter | solution.py:356
  1260.1 162.0 %reduce-scatter.50.cloned.1.call-start = ((), (), s32[]{:S(2)}) async-start(), calls=%async_computation.46 | async-start | bytes 1966080 | tf_op jit(solution)/shard_map/reduce_scatter | solution.py:421
  (331 other events, 9549.8 us)
Sparse Core Ops, SparseCore 0:
  10.2 30.8 all-gather.59
  43.5 30.3 all-gather.61
  78.4 28.4 all-gather.35
  109.2 26.4 all-gather.63
  137.4 35.3 all-gather.65
  174.4 35.1 all-gather.67
  212.6 35.1 reduce-scatter.21
  250.2 27.1 reduce-scatter.25
  337.6 26.5 all-gather.37
  365.6 27.4 all-gather.41
  395.5 25.9 all-gather.39
  423.7 26.4 all-gather.69
  502.7 35.1 reduce-scatter.29
  540.2 27.1 reduce-scatter.27
  639.5 26.5 all-gather.43
  667.5 27.4 all-gather.49
  697.3 25.9 all-gather.45
  725.2 26.4 all-gather.47
  753.5 26.4 all-gather.71
  781.8 26.4 all-gather.75
  852.4 35.2 reduce-scatter.37
  890.0 27.1 reduce-scatter.41
  978.5 26.5 all-gather.51
  1006.5 27.4 all-gather.57
  1064.2 26.4 all-gather.53
  1092.4 26.4 all-gather.73
  1120.7 26.4 all-gather.77
  1191.7 35.1 reduce-scatter.43
  1258.0 35.1 reduce-scatter.55
  1296.5 35.1 reduce-scatter.53
  1333.9 27.1 reduce-scatter.47
  1392.3 29.8 reduce-scatter.49
  (9 shorter events, 230.9 us)
where the time goes:
time: 1440 us; the launch traced here: 1430 us
  waiting for transfers between devices  701 us (49%)
  matrix products  370 us (26%)
  other arithmetic  137 us (10%)
  local copies, waits for them, and re-layouts  105 us (7%)
  blocking collectives  94.6 us (7%)
  between operations  19.1 us (1%)
    reduce_scatter x4, waiting for transfers between devices, body(): lax.psum_scatter(grad_normed_a.astype(jnp.bfloat16), 'col', scatter_dimen...  113 us
    reduce_scatter x4, waiting for transfers between devices, body(): lax.psum_scatter(grad_normed_m.astype(jnp.bfloat16), 'col', scatter_dimen...  81.1 us
    all_gather x4, waiting for transfers between devices, body(): lax.all_gather(key_flat, 'row', axis=0, tiled=True)  78.2 us
    all_gather x4, waiting for transfers between devices, body(): gathered = lax.all_gather(layer_entry_input, 'col', axis=1, tiled=True)  74.6 us
    all_gather x4, waiting for transfers between devices, body(): lax.all_gather(value_flat, 'row', axis=0, tiled=True)  62.4 us
    reduce_scatter x3, waiting for transfers between devices, body(): lax.psum_scatter(branch_terms.astype(jnp.bfloat16), 'col', scatter_dimens...  54.5 us
    dot_general x16, matrix products, body(): jnp.einsum('qhd,khd->hqk', grad_out3, value_part, preferred_element_type=...  47.4 us
    dot_general x16, matrix products, body(): jnp.einsum('hqk,qhd->khd', probs.astype(jnp.bfloat16), grad_out3, preferr...  42.9 us
  transfers between devices with their start and end apart: 44, of which 38 were waited for; matrix products, arithmetic and copies ran while one was open for 29% of the time, Pallas kernels for 0%

commit v1 on v0

v1 whole, which is shorter than its diff:
```python
from functools import partial
import math

import jax
import jax.numpy as jnp
from jax import lax
from jax.experimental import pallas as pl
from jax.experimental.pallas import tpu as pltpu
from jax.sharding import PartitionSpec as P

MODEL_WIDTH = 1024
HEAD_DIM = 64
ROT = 16


EPS = 1e-05
NEG = -1e30


def from_partner(value, axis, apart):
    mask = 2**apart
    pairs = [(source, source ^ mask) for source in range(lax.axis_size(axis))]
    return lax.ppermute(value, axis, pairs)


def segment_of(token_ids, starts):
    return jnp.sum((token_ids[:, None] >= starts[None, 1:]).astype(jnp.int32), axis=1)


def token_layout(lengths_row, token_ids):
    starts = jnp.cumsum(lengths_row) - lengths_row
    segment = segment_of(token_ids, starts)
    labels = jnp.arange(1, lengths_row.shape[0], dtype=jnp.int32)
    seg_begin = jnp.sum(jnp.where(segment[:, None] == labels[None, :], starts[None, 1:], 0), axis=1)
    position = jnp.where(segment == 0, token_ids, lengths_row[0] + token_ids - seg_begin)
    return (starts, segment, position)


def rotary_tables(position, turned):
    half_rot = turned // 2
    freqs = 10000.0 ** (-(2.0 * jnp.arange(half_rot, dtype=jnp.float32)) / turned)
    angles = position.astype(jnp.float32)[:, None] * freqs[None, :]
    return (jnp.cos(angles), jnp.sin(angles))


def rotate(values, cos_table, sin_table, direction):
    half_rot = cos_table.shape[-1]
    lower = values[..., :half_rot]
    upper = values[..., half_rot : 2 * half_rot]
    cos_cast = cos_table[:, None, :]
    sin_cast = direction * sin_table[:, None, :]
    return jnp.concatenate(
        [
            lower * cos_cast - upper * sin_cast,
            upper * cos_cast + lower * sin_cast,
            values[..., 2 * half_rot :],
        ],
        axis=-1,
    )


def permitted(query_seg, query_tok, key_seg, key_tok):
    from_prompt = (key_seg[None, :] == 0) & (query_seg[:, None] > 0)
    same_causal = (key_seg[None, :] == query_seg[:, None]) & (
        key_tok[None, :] <= query_tok[:, None]
    )
    return from_prompt | same_causal


def attend(running, key_piece, value_piece, query3, layout):
    run_max, run_sum, totals = running
    piece_len = key_piece.shape[0]
    key3 = key_piece.reshape(piece_len, query3.shape[1], query3.shape[2])
    value3 = value_piece.reshape(piece_len, query3.shape[1], query3.shape[2])
    key_tok = jnp.arange(piece_len, dtype=jnp.int32)
    key_seg = segment_of(key_tok, layout["starts"])
    allowed = permitted(layout["segment"], layout["tokens"], key_seg, key_tok)[None]
    scores = jnp.einsum("qhd,khd->hqk", query3, key3, preferred_element_type=jnp.float32) * (
        1.0 / math.sqrt(query3.shape[2])
    )
    masked = jnp.where(allowed, scores, NEG)
    new_max = jnp.maximum(run_max, jnp.max(masked, axis=-1))
    weights = jnp.where(allowed, jnp.exp(masked - new_max[..., None]), 0.0)
    run_sum = jnp.sum(weights, axis=-1)
    totals = jnp.einsum(
        "hqk,khd->hqd", weights.astype(jnp.bfloat16), value3, preferred_element_type=jnp.float32
    )
    return (new_max, run_sum, totals)


def layer_forward(x, full, weights, layout, complete_gains, complete_shifts):
    w_query, b_query, w_output, w_hidden, b_hidden, w_project, b_output = weights
    row_tokens, local_width = x.shape
    heads_local = local_width // HEAD_DIM
    shaped = (row_tokens, heads_local, HEAD_DIM)
    as_float = full.astype(jnp.float32)
    row_mean = jnp.mean(as_float, axis=1, keepdims=True)
    centred = as_float - row_mean
    rstd = lax.rsqrt(jnp.mean(centred * centred, axis=1, keepdims=True) + EPS)
    unit = centred * rstd
    normed_a = (unit * complete_gains[0] + complete_shifts[0]).astype(jnp.bfloat16)
    normed_m = (unit * complete_gains[1] + complete_shifts[1]).astype(jnp.bfloat16)
    projected = (
        jnp.einsum("td,cde->cte", normed_a, w_query, preferred_element_type=jnp.float32)
        + b_query[:, None, :]
    )
    cos_table, sin_table = layout["cos_table"], layout["sin_table"]
    query3 = rotate(projected[0].reshape(shaped), cos_table, sin_table, 1.0).astype(jnp.bfloat16)
    key_flat = (
        rotate(projected[1].reshape(shaped), cos_table, sin_table, 1.0)
        .reshape(row_tokens, local_width)
        .astype(jnp.bfloat16)
    )
    value_flat = projected[2].astype(jnp.bfloat16)
    key_full = lax.all_gather(key_flat, "row", axis=0, tiled=True)
    value_full = lax.all_gather(value_flat, "row", axis=0, tiled=True)
    initial = (
        jnp.full((heads_local, row_tokens), NEG, jnp.float32),
        jnp.zeros((heads_local, row_tokens), jnp.float32),
        jnp.zeros((heads_local, row_tokens, HEAD_DIM), jnp.float32),
    )
    run_max, run_sum, totals = attend(initial, key_full, value_full, query3, layout)
    out_exact = totals / run_sum[..., None]
    log_sum = run_max + jnp.log(run_sum)
    attn_flat = (
        jnp.transpose(out_exact, (1, 0, 2)).reshape(row_tokens, local_width).astype(jnp.bfloat16)
    )
    hidden_pre = jnp.dot(normed_m, w_hidden, preferred_element_type=jnp.float32) + b_hidden
    hidden = jax.nn.gelu(hidden_pre, approximate=False).astype(jnp.bfloat16)
    branch = jnp.dot(attn_flat, w_output, preferred_element_type=jnp.float32) + jnp.dot(
        hidden, w_project, preferred_element_type=jnp.float32
    )
    summed = lax.psum_scatter(
        branch.astype(jnp.bfloat16), "col", scatter_dimension=1, tiled=True
    ).astype(jnp.float32)
    output = (x.astype(jnp.float32) + summed + b_output).astype(jnp.bfloat16)
    state = dict(
        unit=unit, rstd=rstd, normed_a=normed_a, normed_m=normed_m, query3=query3,
        key_full=key_full, value_full=value_full, attn_flat=attn_flat, out_exact=out_exact,
        log_sum=log_sum, hidden_pre=hidden_pre, hidden=hidden,
    )
    return output, state


def layer_backward(state, grad_in, grad_full, weights, layout, complete_gains, scatter_tokens):
    w_query, b_query, w_output, w_hidden, b_hidden, w_project, b_output = weights
    row_tokens = state["normed_a"].shape[0]
    local_width = w_output.shape[0]
    heads_local = local_width // HEAD_DIM
    shaped = (row_tokens, heads_local, HEAD_DIM)
    score_scale = 1.0 / math.sqrt(HEAD_DIM)
    total_tokens = state["key_full"].shape[0]
    key_block = min(512, total_tokens)
    grad_wout = jnp.einsum(
        "te,td->ed", state["attn_flat"], grad_full, preferred_element_type=jnp.float32
    )
    grad_wproj = jnp.einsum(
        "tf,td->fd", state["hidden"], grad_full, preferred_element_type=jnp.float32
    )
    grad_bout = jnp.sum(grad_in.astype(jnp.float32), axis=0)
    grad_attn = jnp.einsum(
        "td,ed->te", grad_full, w_output, preferred_element_type=jnp.float32
    ).astype(jnp.bfloat16)
    grad_hidden = jnp.einsum("td,fd->tf", grad_full, w_project, preferred_element_type=jnp.float32)
    gelu_value, gelu_back = jax.vjp(partial(jax.nn.gelu, approximate=False), state["hidden_pre"])
    grad_hpre = gelu_back(grad_hidden)[0].astype(jnp.bfloat16)
    grad_wfc = jnp.einsum(
        "td,tf->df", state["normed_m"], grad_hpre, preferred_element_type=jnp.float32
    )
    grad_bfc = jnp.sum(grad_hpre.astype(jnp.float32), axis=0)
    grad_normed_m = jnp.einsum("tf,df->td", grad_hpre, w_hidden, preferred_element_type=jnp.float32)
    grad_out3 = grad_attn.reshape(shaped)
    query3 = state["query3"]
    delta = jnp.sum(
        jnp.transpose(grad_out3.astype(jnp.float32), (1, 0, 2)) * state["out_exact"], axis=-1
    )
    grad_query = jnp.zeros(shaped, jnp.float32)
    key_terms = []
    value_terms = []
    for block_no in range(total_tokens // key_block):
        begin_at = block_no * key_block
        key_part = state["key_full"][begin_at : begin_at + key_block].reshape(
            key_block, heads_local, HEAD_DIM
        )
        value_part = state["value_full"][begin_at : begin_at + key_block].reshape(
            key_block, heads_local, HEAD_DIM
        )
        key_tok = begin_at + jnp.arange(key_block, dtype=jnp.int32)
        key_seg = segment_of(key_tok, layout["starts"])
        allowed = permitted(layout["segment"], layout["tokens"], key_seg, key_tok)[None]
        scores = (
            jnp.einsum("qhd,khd->hqk", query3, key_part, preferred_element_type=jnp.float32)
            * score_scale
        )
        probs = jnp.where(
            allowed,
            jnp.exp(jnp.where(allowed, scores, NEG) - state["log_sum"][..., None]),
            0.0,
        )
        grad_probs = jnp.einsum(
            "qhd,khd->hqk", grad_out3, value_part, preferred_element_type=jnp.float32
        )
        grad_scores = (probs * (grad_probs - delta[..., None])).astype(jnp.bfloat16)
        grad_query = grad_query + jnp.einsum(
            "hqk,khd->qhd", grad_scores, key_part, preferred_element_type=jnp.float32
        )
        key_terms.append(
            jnp.einsum(
                "hqk,qhd->khd", grad_scores, query3, preferred_element_type=jnp.float32
            ).reshape(key_block, local_width)
            * score_scale
        )
        value_terms.append(
            jnp.einsum(
                "hqk,qhd->khd",
                probs.astype(jnp.bfloat16),
                grad_out3,
                preferred_element_type=jnp.float32,
            ).reshape(key_block, local_width)
        )
    grad_query = grad_query * score_scale
    kv_terms = jnp.concatenate(
        [jnp.concatenate(key_terms, axis=0), jnp.concatenate(value_terms, axis=0)], axis=1
    )
    kv_grads = lax.psum_scatter(
        kv_terms.astype(jnp.bfloat16), "row", scatter_dimension=0, tiled=True
    ).astype(jnp.float32)
    grad_key = kv_grads[:, :local_width].reshape(shaped)
    grad_value = kv_grads[:, local_width:]
    cos_table, sin_table = layout["cos_table"], layout["sin_table"]
    grad_pre = jnp.stack(
        [
            rotate(grad_query, cos_table, sin_table, -1.0).reshape(row_tokens, local_width),
            rotate(grad_key, cos_table, sin_table, -1.0).reshape(row_tokens, local_width),
            grad_value,
        ]
    ).astype(jnp.bfloat16)
    grad_wqkv = jnp.einsum(
        "td,cte->cde", state["normed_a"], grad_pre, preferred_element_type=jnp.float32
    )
    grad_bqkv = jnp.sum(grad_pre.astype(jnp.float32), axis=1)
    grad_normed_a = jnp.einsum("cte,cde->td", grad_pre, w_query, preferred_element_type=jnp.float32)
    unit = state["unit"]
    grad_gains = jnp.stack(
        [jnp.sum(grad_normed_a * unit, axis=0), jnp.sum(grad_normed_m * unit, axis=0)]
    )
    grad_shifts = jnp.stack([jnp.sum(grad_normed_a, axis=0), jnp.sum(grad_normed_m, axis=0)])
    grad_unit = grad_normed_a * complete_gains[0] + grad_normed_m * complete_gains[1]
    big = (grad_wqkv, grad_wout, grad_wfc, grad_wproj)
    big = tuple(member.astype(jnp.bfloat16) for member in big)
    shared = (grad_gains, grad_shifts)
    local = (grad_bqkv, grad_bfc, grad_bout)
    if scatter_tokens:
        piece = lax.psum_scatter(
            grad_unit.astype(jnp.bfloat16), "col", scatter_dimension=0, tiled=True
        ).astype(jnp.float32)
        rows = piece.shape[0]
        start = lax.axis_index("col") * rows
        unit_part = lax.dynamic_slice_in_dim(unit, start, rows, 0)
        rstd_part = lax.dynamic_slice_in_dim(state["rstd"], start, rows, 0)
        grad_part = lax.dynamic_slice_in_dim(grad_full, start, rows, 0).astype(jnp.float32)
        moved = (
            piece
            - jnp.mean(piece, axis=1, keepdims=True)
            - unit_part * jnp.mean(piece * unit_part, axis=1, keepdims=True)
        )
        grad_input = (grad_part + rstd_part * moved).astype(jnp.bfloat16)
    else:
        sums = lax.psum(
            jnp.stack([jnp.sum(grad_unit, axis=1), jnp.sum(grad_unit * unit, axis=1)]), "col"
        )
        piece = lax.psum_scatter(
            grad_unit.astype(jnp.bfloat16), "col", scatter_dimension=1, tiled=True
        ).astype(jnp.float32)
        width = piece.shape[1]
        unit_part = lax.dynamic_slice_in_dim(unit, lax.axis_index("col") * width, width, 1)
        moved = (
            piece
            - sums[0][:, None] / MODEL_WIDTH
            - unit_part * (sums[1][:, None] / MODEL_WIDTH)
        )
        grad_input = (grad_in.astype(jnp.float32) + state["rstd"] * moved).astype(jnp.bfloat16)
    return grad_input, big, shared, local


def body(
    hidden_in,
    cotangent,
    lengths,
    norm_gains,
    norm_biases,
    w_qkv,
    b_qkv,
    w_out,
    w_fc,
    b_fc,
    w_proj,
    b_out,
):
    row_tokens = hidden_in.shape[1]
    local_width = hidden_in.shape[2]
    section = lax.axis_index("section")
    is_first = section == 0
    my_tokens = lax.axis_index("row") * row_tokens + jnp.arange(row_tokens, dtype=jnp.int32)
    x0 = lax.dynamic_index_in_dim(hidden_in, section, 0, keepdims=False)
    cot = lax.dynamic_index_in_dim(cotangent, section, 0, keepdims=False)
    lengths_row = lax.dynamic_index_in_dim(lengths, section, 0, keepdims=False)
    starts, segment, position = token_layout(lengths_row, my_tokens)
    cos_table, sin_table = rotary_tables(position, ROT)
    layout = {
        "starts": starts,
        "segment": segment,
        "tokens": my_tokens,
        "cos_table": cos_table,
        "sin_table": sin_table,
    }
    both = ("section", "row")
    gains = lax.all_gather(norm_gains[0], ("section", "col"), axis=0)
    shifts = lax.all_gather(norm_biases[0], ("section", "col"), axis=0)
    cols = lax.axis_size("col")

    def whole(vectors):
        split = vectors.reshape(2, cols, 2, local_width)
        return jnp.transpose(split, (0, 2, 1, 3)).reshape(2, 2, cols * local_width)

    gains, shifts = whole(gains), whole(shifts)
    biases = [lax.all_gather(member[0], "section", axis=0) for member in (b_qkv, b_fc, b_out)]
    x0_full = lax.all_gather(x0, "col", axis=1, tiled=True)
    rows = lax.axis_size("row")

    def unite(member, axis):
        gathered = lax.all_gather(member[0], both, axis=0)
        pieces = gathered.reshape((2, rows) + gathered.shape[1:])
        return [
            jnp.concatenate([pieces[layer, row] for row in range(rows)], axis=axis)
            for layer in range(2)
        ]

    w_query, w_hidden = unite(w_qkv, 1), unite(w_fc, 0)
    w_output, w_project = unite(w_out, 1), unite(w_proj, 1)
    weights = [
        (
            w_query[layer],
            biases[0][layer],
            w_output[layer],
            w_hidden[layer],
            biases[1][layer],
            w_project[layer],
            biases[2][layer],
        )
        for layer in range(2)
    ]
    out0, state0 = layer_forward(x0, x0_full, weights[0], layout, gains[0], shifts[0])
    x1_full = lax.all_gather(out0, "col", axis=1, tiled=True)
    cot_full = lax.all_gather(cot, "col", axis=1, tiled=True)
    out1, state1 = layer_forward(out0, x1_full, weights[1], layout, gains[1], shifts[1])
    grad1_part, big1, shared1, local1 = layer_backward(
        state1, cot, cot_full, weights[1], layout, gains[1], True
    )
    grad1_full = lax.all_gather(grad1_part, "col", axis=0, tiled=True)
    grad1 = lax.dynamic_slice_in_dim(
        grad1_full, lax.axis_index("col") * local_width, local_width, 1
    )
    grad0, big0, shared0, local0 = layer_backward(
        state0, grad1, grad1_full, weights[0], layout, gains[0], False
    )

    def swap(first, second):
        mine = jnp.where(is_first, first, second)
        theirs = from_partner(jnp.where(is_first, second, first), "section", 0)
        return jnp.where(is_first, jnp.stack([mine, theirs]), jnp.stack([theirs, mine]))[None]

    out_rows = swap(out0, out1)
    grad_rows = swap(grad0, grad1)

    def scatter(first, second, axis):
        length = first.shape[axis] // rows
        pieces = jnp.stack(
            [
                lax.slice_in_dim(member, row * length, (row + 1) * length, axis=axis)
                for member in (first, second)
                for row in range(rows)
            ]
        )
        return lax.psum_scatter(pieces, both, scatter_dimension=0, tiled=True).astype(jnp.float32)

    large = [scatter(a, b, axis) for a, b, axis in zip(big0, big1, (1, 1, 0, 1))]
    shared_sums = lax.psum(
        tuple(jnp.stack([a, b]) for a, b in zip(shared0, shared1)), ("section", "row", "col")
    )
    shared_mine = [
        lax.dynamic_slice(
            member,
            (section, 0, lax.axis_index("col") * local_width),
            (1, 2, local_width),
        )
        for member in shared_sums
    ]
    local_sums = lax.psum(tuple(jnp.stack([a, b]) for a, b in zip(local0, local1)), both)
    local_mine = [lax.dynamic_index_in_dim(member, section, 0) for member in local_sums]
    return (
        out_rows,
        grad_rows,
        shared_mine[0],
        shared_mine[1],
        large[0],
        local_mine[0],
        large[1],
        large[2],
        local_mine[1],
        large[3],
        local_mine[2],
    )


BF = jnp.bfloat16
F32 = jnp.float32
BY_MESH = pl.DeviceIdType.MESH
VMEM_LIMIT = 60 * 2**20
ATTENTION_BLOCK = 256
PARTS = 2


def dot(a, b, contract=((1,), (0,))):
    return lax.dot_general(a, b, (contract, ((), ())), preferred_element_type=F32)


def rcopy(src, dst, ssem, rsem, **device):
    return pltpu.make_async_remote_copy(
        src_ref=src,
        dst_ref=dst,
        send_sem=ssem,
        recv_sem=rsem,
        device_id=device,
        device_id_type=BY_MESH,
    )


class Place:
    def __init__(self, rows, cols):
        self.rows, self.cols = rows, cols
        self.s = lax.axis_index("section")
        self.r = lax.axis_index("row")
        self.c = lax.axis_index("col")

    def row_to(self, step):
        return lax.rem(self.r + step, self.rows)

    def row_from(self, step):
        return lax.rem(self.r + self.rows - step, self.rows)

    def col_to(self, step):
        return lax.rem(self.c + step, self.cols)

    def col_from(self, step):
        return lax.rem(self.c + self.cols - step, self.cols)

    def greet(self, rows=False, cols=False, partner=False, cross_cols=False, cross_rows=False):
        barrier = pltpu.get_barrier_semaphore()
        count = 0

        def signal(**device):
            pl.semaphore_signal(barrier, inc=1, device_id=device, device_id_type=BY_MESH)

        if rows:
            for step in range(1, self.rows):
                signal(row=self.row_to(step))
                count += 1
        if cols:
            for step in range(1, self.cols):
                signal(col=self.col_to(step))
                count += 1
        if partner:
            signal(section=1 - self.s)
            count += 1
        if cross_cols:
            for step in range(1, self.cols):
                signal(section=1 - self.s, col=self.col_to(step))
                count += 1
        if cross_rows:
            for step in range(1, self.rows):
                signal(section=1 - self.s, row=self.row_to(step))
                count += 1
        pl.semaphore_wait(barrier, count)


class LineGather:
    def __init__(self, place, view, send_right, send_left, recv, lane=0):
        self.place, self.view, self.lane = place, view, lane
        self.send_right, self.send_left, self.recv = send_right, send_left, recv

    def right(self, block):
        return rcopy(
            self.view(block), self.view(block), self.send_right.at[self.lane, block],
            self.recv.at[self.lane, block],
            col=lax.rem(self.place.c + 1, self.place.cols),
        )

    def left(self, block):
        cols = self.place.cols
        return rcopy(
            self.view(block), self.view(block), self.send_left.at[self.lane, block],
            self.recv.at[self.lane, block],
            col=lax.rem(self.place.c + cols - 1, cols),
        )

    def hop(self, distance):
        c, cols = self.place.c, self.place.cols

        @pl.when(c >= distance)
        def _():
            block = lax.rem(c + cols - distance, cols)
            if distance:
                self.right(block).wait_recv()

            @pl.when(c < cols - 1)
            def _():
                self.right(block).start()

        @pl.when(c + distance < cols)
        def _():
            block = lax.rem(c + distance, cols)
            if distance:
                self.left(block).wait_recv()

            @pl.when(c > 0)
            def _():
                self.left(block).start()

    def finish(self):
        c, cols = self.place.c, self.place.cols
        for distance in range(cols):

            @pl.when((c >= distance) & (c < cols - 1))
            def _():
                self.right(lax.rem(c + cols - distance, cols)).wait_send()

            @pl.when((c + distance < cols) & (c > 0))
            def _():
                self.left(lax.rem(c + distance, cols)).wait_send()


class WeightGather:
    def __init__(self, place, layer, own, full, send, recv, pass_on, local):
        self.place, self.layer, self.own, self.full = place, layer, own, full
        self.send, self.recv, self.pass_on, self.local = send, recv, pass_on, local

    def view(self, kind, block):
        length = self.own[kind].shape[-2 if kind in (0, 1) else -1]
        piece = pl.ds(pl.multiple_of(block * length, length), length)
        if kind == 0:
            return self.full[0].at[:, piece, :]
        if kind == 1:
            return self.full[1].at[piece, :]
        return self.full[kind].at[:, piece]

    def over_row(self, kind, step):
        place = self.place
        return rcopy(
            self.own[kind], self.view(kind, place.r), self.send.at[kind, step],
            self.recv.at[kind, step], row=place.row_to(step),
        )

    def arriving(self, kind, step):
        block = self.view(kind, self.place.row_from(step))
        return rcopy(
            block, block, self.send.at[kind, step], self.recv.at[kind, step],
            row=self.place.row_to(step),
        )

    def to_partner(self, kind, step):
        place = self.place
        block = self.view(kind, place.row_from(step))
        return rcopy(
            self.own[kind] if step == 0 else block, block, self.pass_on.at[kind, step],
            self.recv.at[kind, step], section=1 - place.s,
        )

    def keep(self, kind):
        return pltpu.make_async_copy(
            self.own[kind], self.view(kind, self.place.r), self.local.at[kind]
        )

    def start(self, kind):
        @pl.when(self.place.s == self.layer)
        def _():
            for step in range(1, self.place.rows):
                self.over_row(kind, step).start()
            self.keep(kind).start()
            self.to_partner(kind, 0).start()

    def forward(self, kind):
        @pl.when(self.place.s == self.layer)
        def _():
            for step in range(1, self.place.rows):
                self.arriving(kind, step).wait_recv()
                self.to_partner(kind, step).start()
            self.keep(kind).wait()

    def ready(self, kind):
        @pl.when(self.place.s != self.layer)
        def _():
            for step in range(self.place.rows):
                self.to_partner(kind, step).wait_recv()

    def finish(self, kind):
        @pl.when(self.place.s == self.layer)
        def _():
            for step in range(1, self.place.rows):
                self.over_row(kind, step).wait_send()
            for step in range(self.place.rows):
                self.to_partner(kind, step).wait_send()


class RowExchange:
    def __init__(self, place, piece_for, slot_of, send, recv, local):
        self.place, self.piece_for, self.slot_of = place, piece_for, slot_of
        self.send, self.recv, self.local = send, recv, local

    def out(self, step):
        place = self.place
        target = place.row_to(step)
        return rcopy(
            self.piece_for(target), self.slot_of(place.r), self.send.at[step], self.recv.at[step],
            row=target,
        )

    def into(self, step):
        slot = self.slot_of(self.place.row_from(step))
        return rcopy(
            slot, slot, self.send.at[step], self.recv.at[step], row=self.place.row_to(step)
        )

    def keep(self):
        return pltpu.make_async_copy(
            self.piece_for(self.place.r), self.slot_of(self.place.r), self.local
        )

    def start(self):
        for step in range(1, self.place.rows):
            self.out(step).start()
        self.keep().start()

    def arrive(self):
        for step in range(1, self.place.rows):
            self.into(step).wait_recv()
        self.keep().wait()

    def finish(self):
        for step in range(1, self.place.rows):
            self.out(step).wait_send()


def norm_rows(source, gains_a, shifts_a, gains_m, shifts_m, normed_a, normed_m):
    tokens = source.shape[0]
    tile = min(128, tokens)

    @pl.loop(0, tokens // tile)
    def _(index):
        rows = pl.ds(pl.multiple_of(index * tile, tile), tile)
        values = source[rows, :].astype(F32)
        centred = values - jnp.mean(values, axis=1, keepdims=True)
        unit = centred * lax.rsqrt(jnp.mean(centred * centred, axis=1, keepdims=True) + EPS)
        normed_a[rows, :] = (unit * gains_a + shifts_a).astype(BF)
        normed_m[rows, :] = (unit * gains_m + shifts_m).astype(BF)


def turn(block, cos, sin, direction):
    half = cos.shape[0]
    lower, upper, rest = block[:half], block[half : 2 * half], block[2 * half :]
    return jnp.concatenate(
        [
            lower * cos - upper * (direction * sin),
            upper * cos + lower * (direction * sin),
            rest,
        ],
        axis=0,
    )


def project_heads(normed_a, w_query, bias_rows, cos, sin, pieces, heads):
    for kind in range(3):
        values = dot(normed_a[...], w_query[kind]) + bias_rows(kind)
        flipped = values.T
        for head in range(heads):
            block = flipped[head * HEAD_DIM : (head + 1) * HEAD_DIM]
            if kind < 2:
                block = turn(block, cos[...], sin[...], 1.0)
            pieces[head, kind * HEAD_DIM : (kind + 1) * HEAD_DIM, :] = block.astype(BF)


def feed_forward(normed_m, w_hidden, bias_of, hidden, slope):
    tile = min(256, w_hidden.shape[1])

    @pl.loop(0, w_hidden.shape[1] // tile)
    def _(index):
        cols = pl.ds(pl.multiple_of(index * tile, tile), tile)
        pre = dot(normed_m[...], w_hidden[:, cols]) + bias_of(index)
        phi = 0.5 * (1.0 + lax.erf(pre * math.sqrt(0.5)))
        hidden[:, cols] = (pre * phi).astype(BF)
        slope[:, cols] = phi + pre * (jnp.exp(-0.5 * pre * pre) * (1.0 / math.sqrt(2.0 * math.pi)))


def times_tiles(left, right, out, convert=None, contract=((1,), (0,))):
    tile = min(256, out.shape[1])

    @pl.loop(0, out.shape[1] // tile)
    def _(index):
        cols = pl.ds(pl.multiple_of(index * tile, tile), tile)
        piece = right[:, cols] if contract[1] == (0,) else right[cols, :]
        value = dot(left[...], piece, contract)
        out[:, cols] = value if convert is None else convert(value, cols)


def opening_kernel(
    rows, cols,
    hidden_in, cotangent, vectors, wq, wf, wo, wp, cos, sin,
    x_full, cot_full, vec_all, wq_all, wf_all, wo_all, wp_all, normed_a, normed_m, qkv, hidden, slope, branch,
    pieces,
    xr, xl, xv, cr, cl, cv, vs, vr, ws, wr, wpas, wloc, as_, ar, local,
):
    place = Place(rows, cols)
    s, c = place.s, place.c
    width = hidden_in.shape[2]

    def cols_of(ref):
        return lambda block: ref.at[:, pl.ds(pl.multiple_of(block * width, width), width)]

    def vec_slot(section, col):
        return vec_all.at[section, :, pl.ds(pl.multiple_of(col * width, width), width)]

    def vec_copy(ds, dc):
        index = ds * cols + dc
        return rcopy(
            vectors, vec_slot(s, c), vs.at[index], vr.at[index],
            section=lax.rem(s + ds, 2), col=place.col_to(dc),
        )

    def vec_into(ds, dc):
        index = ds * cols + dc
        slot = vec_slot(lax.rem(s + ds, 2), place.col_from(dc))
        return rcopy(
            slot, slot, vs.at[index], vr.at[index],
            section=lax.rem(s + ds, 2), col=place.col_to(dc),
        )

    others = [(ds, dc) for ds in range(2) for dc in range(cols) if ds or dc]
    x_own = pltpu.make_async_copy(hidden_in.at[s], cols_of(x_full)(c), local.at[0])
    c_own = pltpu.make_async_copy(cotangent.at[s], cols_of(cot_full)(c), local.at[1])
    v_own = pltpu.make_async_copy(vectors, vec_slot(s, c), local.at[2])
    for copy in (x_own, c_own, v_own):
        copy.start()
    place.greet(rows=True, cols=True, partner=True, cross_cols=True)
    weights = WeightGather(
        place, 0, (wq, wf, wo, wp), (wq_all, wf_all, wo_all, wp_all), ws, wr, wpas, wloc
    )
    x_gather = LineGather(place, cols_of(x_full), xr, xl, xv)
    c_gather = LineGather(place, cols_of(cot_full), cr, cl, cv)
    x_own.wait()
    x_gather.hop(0)
    for ds, dc in others:
        vec_copy(ds, dc).start()
    weights.start(0)
    x_gather.hop(1)
    weights.forward(0)
    weights.start(1)
    for distance in range(2, cols):
        x_gather.hop(distance)
    c_own.wait()
    c_gather.hop(0)
    v_own.wait()
    for ds, dc in others:
        vec_into(ds, dc).wait_recv()

    def row(index):
        return vec_all[0, index : index + 1, :]

    own = pl.ds(pl.multiple_of(c * width, width), width)
    norm_rows(x_full, row(0), row(2), row(1), row(3), normed_a, normed_m)
    weights.ready(0)
    project_heads(
        normed_a, wq_all, lambda kind: vec_all[0, 4 + kind : 5 + kind, own], cos, sin, pieces, rows
    )
    tokens = normed_a.shape[0]
    exchange = RowExchange(
        place,
        lambda target: pieces.at[target],
        lambda source: qkv.at[:, pl.ds(pl.multiple_of(source * tokens, tokens), tokens)],
        as_, ar, local.at[3],
    )
    exchange.start()
    weights.forward(1)
    weights.start(3)
    weights.start(2)
    c_gather.hop(1)
    weights.ready(1)
    feed_forward(
        normed_m, wf_all, lambda index: vec_all[0, pl.ds(8 + index, 1), own], hidden, slope
    )
    for distance in range(2, cols):
        c_gather.hop(distance)
    exchange.arrive()
    weights.forward(3)
    weights.forward(2)
    weights.ready(3)
    times_tiles(hidden, wp_all, branch)
    weights.ready(2)
    x_gather.finish()
    c_gather.finish()
    exchange.finish()
    for ds, dc in others:
        vec_copy(ds, dc).wait_send()
    for kind in range(4):
        weights.finish(kind)


def kernel_call(kernel, collective_id, outs, scratch, *args, cost=None):
    vmem = pl.BlockSpec(memory_space=pltpu.VMEM)
    return pl.pallas_call(
        kernel,
        out_shape=[jax.ShapeDtypeStruct(shape, dtype) for shape, dtype in outs],
        in_specs=[vmem] * len(args),
        out_specs=[vmem] * len(outs),
        scratch_shapes=scratch,
        compiler_params=pltpu.CompilerParams(
            collective_id=collective_id, has_side_effects=True, vmem_limit_bytes=VMEM_LIMIT
        ),
    )(*args)


def dma(*shape):
    return pltpu.SemaphoreType.DMA(shape)


def opening(rows, cols, hidden_in, cotangent, vectors, wq, wf, wo, wp, cos, sin):
    tokens, width = hidden_in.shape[1:]
    full = cols * width
    units = wf.shape[1]
    outs = [
        ((tokens, full), BF),
        ((tokens, full), BF),
        ((2,) + vectors.shape[:1] + (full,), F32),
        ((3, full, width), BF),
        ((full, units), BF),
        ((width, full), BF),
        ((units, full), BF),
        ((tokens, full), BF),
        ((tokens, full), BF),
        ((3 * HEAD_DIM, rows * tokens), BF),
        ((tokens, units), BF),
        ((tokens, units), F32),
        ((tokens, full), F32),
    ]
    scratch = (
        [pltpu.VMEM((rows, 3 * HEAD_DIM, tokens), BF)]
        + [dma(1, cols)] * 6
        + [dma(2 * cols)] * 2
        + [dma(4, rows)] * 3
        + [dma(4)]
        + [dma(rows)] * 2
        + [dma(4)]
    )
    return kernel_call(
        partial(opening_kernel, rows, cols), 1, outs, scratch,
        hidden_in, cotangent, vectors, wq, wf, wo, wp, cos, sin,
    )


def key_mask(prompt, first_ref, cols, key_at, query_at, keys, queries):
    key = lax.broadcasted_iota(jnp.int32, (keys, queries), 0) + key_at
    query = lax.broadcasted_iota(jnp.int32, (keys, queries), 1) + query_at
    return ((key < prompt) | (key >= first_ref[:, cols])) & (key <= query)


def forward_pass(block, prompt, first, qkv, key_rows, out, out_low, log_sum):
    total = qkv.shape[1]

    @pl.loop(0, total // block)
    def _(j):
        query_at = pl.multiple_of(j * block, block)
        cols = pl.ds(query_at, block)
        query = qkv[:HEAD_DIM, cols]

        def step(i, carry):
            top, weight, totals = carry
            key_at = pl.multiple_of(i * block, block)
            scores = dot(key_rows[pl.ds(key_at, block), :], query) * (1.0 / math.sqrt(HEAD_DIM))
            allowed = key_mask(prompt, first, cols, key_at, query_at, block, block)
            scores = jnp.where(allowed, scores, NEG)
            new_top = jnp.maximum(top, jnp.max(scores, axis=0, keepdims=True))
            probs = jnp.exp(scores - new_top)
            fade = jnp.exp(top - new_top)
            weight = weight * fade + jnp.sum(probs, axis=0, keepdims=True)
            value = qkv[2 * HEAD_DIM : 3 * HEAD_DIM, pl.ds(key_at, block)]
            totals = totals * fade + dot(value, probs.astype(BF))
            return new_top, weight, totals

        top, weight, totals = lax.fori_loop(
            0,
            j + 1,
            step,
            (
                jnp.full((1, block), NEG, F32),
                jnp.zeros((1, block), F32),
                jnp.zeros((HEAD_DIM, block), F32),
            ),
        )
        exact = totals / weight
        out[:, cols] = exact
        out_low[:HEAD_DIM, cols] = exact.astype(BF)
        log_sum[:, cols] = top + jnp.log(weight)


def backward_pass(block, prompt, first, qkv, d_out, out, log_sum, key_rows, value_rows, key_acc, value_acc, grads, at):
    total = qkv.shape[1]
    scale = 1.0 / math.sqrt(HEAD_DIM)
    key_acc[...] = jnp.zeros_like(key_acc)
    value_acc[...] = jnp.zeros_like(value_acc)

    @pl.loop(0, total // block)
    def _(j):
        query_at = pl.multiple_of(j * block, block)
        cols = pl.ds(query_at, block)
        query = qkv[:HEAD_DIM, cols]
        d_query = d_out[:, cols]
        delta = jnp.sum(d_query.astype(F32) * out[:, cols], axis=0, keepdims=True)
        log_row = log_sum[:, cols]

        def step(i, d_sum):
            key_at = pl.multiple_of(i * block, block)
            keys = pl.ds(key_at, block)
            scores = dot(key_rows[keys, :], query) * scale
            allowed = key_mask(prompt, first, cols, key_at, query_at, block, block)
            probs = jnp.exp(jnp.where(allowed, scores, NEG) - log_row)
            d_probs = dot(value_rows[keys, :], d_query)
            d_scores = (probs * (d_probs - delta)).astype(BF)
            probs_low = probs.astype(BF)
            key_acc[:, keys] += dot(query, d_scores, ((1,), (1,)))
            value_acc[:, keys] += dot(d_query, probs_low, ((1,), (1,)))
            return d_sum + dot(qkv[HEAD_DIM : 2 * HEAD_DIM, keys], d_scores)

        d_sum = lax.fori_loop(0, j + 1, step, jnp.zeros((HEAD_DIM, block), F32))
        grads[at : at + HEAD_DIM, cols] = (d_sum * scale).astype(BF)

    grads[at + HEAD_DIM : at + 2 * HEAD_DIM, :] = (key_acc[...] * scale).astype(BF)
    grads[at + 2 * HEAD_DIM : at + 3 * HEAD_DIM, :] = value_acc[...].astype(BF)


def rows_of_keys(qkv, at, rows):
    rows[...] = qkv[at : at + HEAD_DIM, :].astype(F32).T.astype(BF)


def attention_forward_kernel(block, lengths, first, qkv, out, out_low, log_sum, key_rows):
    rows_of_keys(qkv, HEAD_DIM, key_rows)
    forward_pass(block, lengths[0], first, qkv, key_rows, out, out_low, log_sum)


def attention_backward_kernel(
    block, lengths, first, qkv, d_out, out, log_sum, grads, key_rows, value_rows, key_acc, value_acc
):
    rows_of_keys(qkv, HEAD_DIM, key_rows)
    rows_of_keys(qkv, 2 * HEAD_DIM, value_rows)
    backward_pass(
        block, lengths[0], first, qkv, d_out, out, log_sum, key_rows, value_rows, key_acc,
        value_acc, grads, 0,
    )


def attention_both_kernel(
    block, lengths, first, qkvd, result, out, log_sum, key_rows, value_rows, key_acc, value_acc
):
    rows_of_keys(qkvd, HEAD_DIM, key_rows)
    rows_of_keys(qkvd, 2 * HEAD_DIM, value_rows)
    forward_pass(block, lengths[0], first, qkvd, key_rows, out, result, log_sum)
    backward_pass(
        block, lengths[0], first, qkvd, qkvd.at[3 * HEAD_DIM :], out, log_sum, key_rows,
        value_rows, key_acc, value_acc, result, HEAD_DIM,
    )


def attention_call(kernel, outs, scratch, lengths, *args):
    vmem = pl.BlockSpec(memory_space=pltpu.VMEM)
    total = args[0].shape[1]
    return pl.pallas_call(
        partial(kernel, min(ATTENTION_BLOCK, total)),
        out_shape=[jax.ShapeDtypeStruct(shape, dtype) for shape, dtype in outs],
        in_specs=[pl.BlockSpec(memory_space=pltpu.SMEM)] + [vmem] * len(args),
        out_specs=[vmem] * len(outs),
        scratch_shapes=[pltpu.VMEM(shape, dtype) for shape, dtype in scratch],
        compiler_params=pltpu.CompilerParams(vmem_limit_bytes=VMEM_LIMIT),
    )(lengths, *args)


def attention_forward(lengths, first, qkv):
    total = qkv.shape[1]
    outs = [((HEAD_DIM, total), F32), ((HEAD_DIM, total), BF), ((1, total), F32)]
    scratch = [((total, HEAD_DIM), BF)]
    return attention_call(attention_forward_kernel, outs, scratch, lengths, first, qkv)


def attention_backward(lengths, first, qkv, d_out, out, log_sum):
    total = qkv.shape[1]
    outs = [((3 * HEAD_DIM, total), BF)]
    scratch = [((total, HEAD_DIM), BF)] * 2 + [((HEAD_DIM, total), F32)] * 2
    return attention_call(
        attention_backward_kernel, outs, scratch, lengths, first, qkv, d_out, out, log_sum
    )[0]


def attention_both(lengths, first, qkvd):
    total = qkvd.shape[1]
    outs = [((4 * HEAD_DIM, total), BF)]
    scratch = (
        [((HEAD_DIM, total), F32), ((1, total), F32)]
        + [((total, HEAD_DIM), BF)] * 2
        + [((HEAD_DIM, total), F32)] * 2
    )
    return attention_call(attention_both_kernel, outs, scratch, lengths, first, qkvd)[0]


class LineReduce:
    def __init__(self, place, total, low, from_left, from_right, view, sems, lane=0):
        self.place, self.total, self.low, self.view, self.lane = place, total, low, view, lane
        self.from_left, self.from_right = from_left, from_right
        self.send_right, self.send_left, self.recv_left, self.recv_right = sems

    def right(self, owner):
        return rcopy(
            self.low.at[self.view(owner)], self.from_left.at[self.view(owner)],
            self.send_right.at[self.lane, owner], self.recv_left.at[self.lane, owner],
            col=lax.rem(self.place.c + 1, self.place.cols),
        )

    def left(self, owner):
        cols = self.place.cols
        return rcopy(
            self.low.at[self.view(owner)], self.from_right.at[self.view(owner)],
            self.send_left.at[self.lane, owner], self.recv_right.at[self.lane, owner],
            col=lax.rem(self.place.c + cols - 1, cols),
        )

    def add_in(self, owner, arrived):
        view = self.view(owner)
        self.low[view] = (self.total[view] + arrived[view].astype(F32)).astype(BF)

    def step(self, time):
        c, cols = self.place.c, self.place.cols

        @pl.when(c <= time)
        def _():
            owner = cols - 1 - time + c

            @pl.when(c > 0)
            def _():
                self.right(owner).wait_recv()
                self.add_in(owner, self.from_left)

            self.right(owner).start()

        @pl.when(c >= cols - 1 - time)
        def _():
            owner = time + c - (cols - 1)

            @pl.when(c < cols - 1)
            def _():
                self.left(owner).wait_recv()
                self.add_in(owner, self.from_right)

            self.left(owner).start()

    def own(self):
        c, cols = self.place.c, self.place.cols
        view = self.view(c)

        @pl.when(c > 0)
        def _():
            self.right(c).wait_recv()

        @pl.when(c == 0)
        def _():
            self.from_left[view] = jnp.zeros_like(self.from_left[view])

        @pl.when(c < cols - 1)
        def _():
            self.left(c).wait_recv()

        @pl.when(c == cols - 1)
        def _():
            self.from_right[view] = jnp.zeros_like(self.from_right[view])

        return (
            self.total[view] + self.from_left[view].astype(F32) + self.from_right[view].astype(F32)
        )

    def finish(self):
        c, cols = self.place.c, self.place.cols
        for time in range(cols - 1):

            @pl.when(c <= time)
            def _():
                self.right(cols - 1 - time + c).wait_send()

            @pl.when(c >= cols - 1 - time)
            def _():
                self.left(time + c - (cols - 1)).wait_send()


def line_sum(place, total, low, from_left, from_right, full, sems, gather_sems, parts, produce, work):
    cols = place.cols
    length = total.shape[0] // cols
    piece = length // parts

    def rows(owner, lane):
        return pl.ds(pl.multiple_of(owner * length + lane * piece, piece), piece)

    reduces = [
        LineReduce(
            place, total, low, from_left, from_right,
            lambda owner, lane=lane: (rows(owner, lane), slice(None)), sems, lane,
        )
        for lane in range(parts)
    ]
    gathers = [
        LineGather(
            place, lambda block, lane=lane: full.at[rows(block, lane), :], *gather_sems, lane=lane
        )
        for lane in range(parts)
    ]
    for time in range(parts * (cols - 1) + cols):
        for lane in reversed(range(parts)):
            phase = time - lane * (cols - 1)
            if 0 <= phase < cols - 1:
                reduces[lane].step(phase)
            elif phase == cols - 1:
                mine = rows(place.c, lane)
                full[mine, :] = produce(reduces[lane].own(), mine)
                gathers[lane].hop(0)
            elif cols - 1 < phase <= 2 * (cols - 1):
                gathers[lane].hop(phase - (cols - 1))
        work(time)
    for lane in range(parts):
        reduces[lane].finish()
        gathers[lane].finish()


class GradExchange:
    def __init__(self, place, layer, mine, theirs, inbox, hand, hand_recv, send, recv):
        self.place, self.layer, self.mine, self.theirs, self.inbox = place, layer, mine, theirs, inbox
        self.hands, self.hand_recv, self.send, self.recv = hand, hand_recv, send, recv
        self.order = tuple(range(1, place.rows)) + (0,)

    def view(self, kind, block):
        length = self.inbox[kind].shape[-2 if kind in (0, 1) else -1]
        piece = pl.ds(pl.multiple_of(block * length, length), length)
        return {
            0: (slice(None), piece, slice(None)),
            1: (piece, slice(None)),
            2: (slice(None), piece),
            3: (slice(None), piece),
        }[kind]

    def passing(self, kind, step):
        view = self.view(kind, self.place.row_to(step))
        return rcopy(
            self.mine[kind].at[view], self.theirs[kind].at[view], self.hands.at[kind, step],
            self.hand_recv.at[kind, step], section=1 - self.place.s,
        )

    def sending(self, kind, step):
        view = self.view(kind, self.place.row_to(step))
        return rcopy(
            self.mine[kind].at[view], self.inbox[kind].at[step], self.send.at[kind, step],
            self.recv.at[kind, step], row=self.place.row_to(step),
        )

    def hand(self, kind):
        @pl.when(self.place.s != self.layer)
        def _():
            for step in self.order:
                self.passing(kind, step).start()

    def merge(self, kind):
        @pl.when(self.place.s == self.layer)
        def _():
            for step in self.order[:-1]:
                self.passing(kind, step).wait_recv()
                view = self.view(kind, self.place.row_to(step))
                self.mine[kind][view] = (
                    self.mine[kind][view].astype(F32) + self.theirs[kind][view].astype(F32)
                ).astype(BF)
                self.sending(kind, step).start()

    def take(self, kind, out):
        @pl.when(self.place.s == self.layer)
        def _():
            self.passing(kind, 0).wait_recv()
            view = self.view(kind, self.place.r)
            total = self.mine[kind][view].astype(F32) + self.theirs[kind][view].astype(F32)
            for step in self.order[:-1]:
                self.sending(kind, step).wait_recv()
                total = total + self.inbox[kind][step].astype(F32)
            out[...] = total

    def finish(self, kind):
        @pl.when(self.place.s == self.layer)
        def _():
            for step in self.order[:-1]:
                self.sending(kind, step).wait_send()

        @pl.when(self.place.s != self.layer)
        def _():
            for step in self.order:
                self.passing(kind, step).wait_send()


def unit_rows(values):
    centred = values - jnp.mean(values, axis=1, keepdims=True)
    rstd = lax.rsqrt(jnp.mean(centred * centred, axis=1, keepdims=True) + EPS)
    return centred * rstd, rstd


def middle_kernel(
    rows, cols,
    attn, wo0, branch0, x_full, vec_all, wq, wf, wo, wp, cot_full, cos, sin,
    attn_t, x1_full, wq_all, wf_all, wo_all, wp_all, normed_a, normed_m, qkvd, hidden, d_pre, branch, d_normed,
    total, low, from_left, from_right, pieces, slope,
    back_s, back_r, rs_a, rs_b, rs_c, rs_d, ag_a, ag_b, ag_c, ws, wr, wpas, wloc, as_, ar, local,
):
    place = Place(rows, cols)
    c = place.c
    tokens, full = x_full.shape
    width = full // cols
    place.greet(rows=True, cols=True, partner=True)
    back = RowExchange(
        place,
        lambda target: attn.at[:, pl.ds(pl.multiple_of(target * tokens, tokens), tokens)],
        lambda source: attn_t.at[pl.ds(pl.multiple_of(source * HEAD_DIM, HEAD_DIM), HEAD_DIM), :],
        back_s, back_r, local.at[0],
    )
    back.start()
    weights = WeightGather(
        place, 1, (wq, wf, wo, wp), (wq_all, wf_all, wo_all, wp_all), ws, wr, wpas, wloc
    )
    back.arrive()
    weights.start(0)
    weights.start(2)
    attn_rows = attn_t[...].astype(F32).T.astype(BF)
    tile = min(256, full)
    for at in range(0, full, tile):
        value = branch0[:, at : at + tile] + dot(attn_rows, wo0[:, at : at + tile])
        total[:, at : at + tile] = value
        low[:, at : at + tile] = value.astype(BF)

    def produce(summed, mine):
        return (x_full[mine, :].astype(F32) + summed + vec_all[0, 7:8, :]).astype(BF)

    def work(time):
        if time == 2:
            weights.start(1)
        if time == 4:
            weights.forward(0)
            weights.forward(2)
            weights.start(3)
        if time == 6:
            weights.ready(2)
            flipped = dot(cot_full[...], wo_all[...], ((1,), (1,))).T
            for head in range(rows):
                pieces[head, 3 * HEAD_DIM :, :] = flipped[
                    head * HEAD_DIM : (head + 1) * HEAD_DIM
                ].astype(BF)
        if time == 7:
            weights.forward(1)

    line_sum(
        place, total, low, from_left, from_right, x1_full, (rs_a, rs_b, rs_c, rs_d),
        (ag_a, ag_b, ag_c), PARTS, produce, work,
    )

    def row(index):
        return vec_all[1, index : index + 1, :]

    own = pl.ds(pl.multiple_of(c * width, width), width)
    norm_rows(x1_full, row(0), row(2), row(1), row(3), normed_a, normed_m)
    weights.ready(0)
    project_heads(
        normed_a, wq_all, lambda kind: vec_all[1, 4 + kind : 5 + kind, own], cos, sin, pieces, rows
    )
    exchange = RowExchange(
        place,
        lambda target: pieces.at[target],
        lambda source: qkvd.at[:, pl.ds(pl.multiple_of(source * tokens, tokens), tokens)],
        as_, ar, local.at[1],
    )
    exchange.start()
    weights.ready(1)
    feed_forward(
        normed_m, wf_all, lambda index: vec_all[1, pl.ds(8 + index, 1), own], hidden, slope
    )
    weights.forward(3)
    weights.ready(3)

    def times_slope(value, where):
        return (value * slope[:, where]).astype(BF)

    times_tiles(cot_full, wp_all, d_pre, times_slope, ((1,), (1,)))
    times_tiles(hidden, wp_all, branch)
    times_tiles(d_pre, wf_all, d_normed, None, ((1,), (1,)))
    exchange.arrive()
    exchange.finish()
    back.finish()
    for kind in range(4):
        weights.finish(kind)


def middle(rows, cols, attn, wo0, branch0, x_full, vec_all, wq, wf, wo, wp, cot_full, cos, sin):
    tokens, full = x_full.shape
    width, units = full // cols, wf.shape[1]
    outs = [
        ((width, tokens), BF),
        ((tokens, full), BF),
        ((3, full, width), BF),
        ((full, units), BF),
        ((width, full), BF),
        ((units, full), BF),
        ((tokens, full), BF),
        ((tokens, full), BF),
        ((4 * HEAD_DIM, rows * tokens), BF),
        ((tokens, units), BF),
        ((tokens, units), BF),
        ((tokens, full), F32),
        ((tokens, full), F32),
    ]
    scratch = (
        [
            pltpu.VMEM((tokens, full), F32),
            pltpu.VMEM((tokens, full), BF),
            pltpu.VMEM((tokens, full), BF),
            pltpu.VMEM((tokens, full), BF),
            pltpu.VMEM((rows, 4 * HEAD_DIM, tokens), BF),
            pltpu.VMEM((tokens, units), F32),
        ]
        + [dma(rows)] * 2
        + [dma(PARTS, cols)] * 7
        + [dma(4, rows)] * 3
        + [dma(4)]
        + [dma(rows)] * 2
        + [dma(2)]
    )
    return kernel_call(
        partial(middle_kernel, rows, cols), 2, outs, scratch,
        attn, wo0, branch0, x_full, vec_all, wq, wf, wo, wp, cot_full, cos, sin,
    )


def d_projection(inbox, at, cos, sin, rows, d_pre, small):
    width = rows * HEAD_DIM
    for kind in range(3):
        parts = []
        for head in range(rows):
            start = at + kind * HEAD_DIM
            block = inbox[head, start : start + HEAD_DIM, :].astype(F32)
            parts.append(turn(block, cos[...], sin[...], -1.0) if kind < 2 else block)
        values = jnp.concatenate(parts, axis=0).T.astype(BF)
        d_pre[:, kind * width : (kind + 1) * width] = values
        small[8 + kind : 9 + kind, :] = jnp.sum(values.astype(F32), axis=0, keepdims=True)


def d_norms(source, d_pre, wq, d_normed, gain_a, gain_m, total, low, sums, after=None):
    tokens = source.shape[0]
    width = wq.shape[2]
    tile = min(128, tokens)
    sums[...] = jnp.zeros_like(sums)

    @pl.loop(0, tokens // tile)
    def _(index):
        rows = pl.ds(pl.multiple_of(index * tile, tile), tile)
        d_a = dot(d_pre[rows, :width], wq[0], ((1,), (1,)))
        for kind in range(1, 3):
            d_a += dot(d_pre[rows, kind * width : (kind + 1) * width], wq[kind], ((1,), (1,)))
        d_m = d_normed[rows, :]
        unit, _ = unit_rows(source[rows, :].astype(F32))
        sums[0:1, :] += jnp.sum(d_a * unit, axis=0, keepdims=True)
        sums[1:2, :] += jnp.sum(d_m * unit, axis=0, keepdims=True)
        sums[2:3, :] += jnp.sum(d_a, axis=0, keepdims=True)
        sums[3:4, :] += jnp.sum(d_m, axis=0, keepdims=True)
        joined = d_a * gain_a + d_m * gain_m
        total[rows, :] = joined
        low[rows, :] = joined.astype(BF)
        if after is not None:
            after(rows, joined, unit)


def unit_sums(d_pre, small, width):
    for index in range(d_pre.shape[1] // width):
        piece = d_pre[:, index * width : (index + 1) * width].astype(F32)
        small[12 + index : 13 + index, :] = jnp.sum(piece, axis=0, keepdims=True)


def across_tokens(left, right, out, at=None):
    tile = min(256, left.shape[1])

    @pl.loop(0, left.shape[1] // tile)
    def _(index):
        cols = pl.ds(pl.multiple_of(index * tile, tile), tile)
        value = dot(left[:, cols], right[...], ((0,), (0,))).astype(BF)
        if at is None:
            out[cols, :] = value
        else:
            width = out.shape[2]
            for kind in range(3):
                out[kind, cols, :] = value[:, kind * width : (kind + 1) * width]


def grad_scratch(rows, full, width, units):
    shapes = [(3, full, width), (full, units), (width, full), (units, full)]
    part = full // rows
    pieces = [(3, part, width), (part, units), (width, part), (units, part)]
    return (
        [pltpu.VMEM(shape, BF) for shape in shapes] * 2
        + [pltpu.VMEM((rows,) + shape, BF) for shape in pieces]
        + [dma(4, rows)] * 4
    ), [(shape, F32) for shape in pieces]


def turning_kernel(
    rows, cols,
    back, x1_full, cot_full, vec_all, wq1, wo0, wp0, wf0, normed_a, normed_m, hidden, d_hidden, d_normed, slope0, cos, sin,
    attn_t, grad_full, d_out, d_hidden0, d_normed0, sums, small, gw_q, gw_f, gw_o, gw_p,
    inbox, d_pre, total, low, from_left, from_right, pieces,
    m0, m1, m2, m3, t0, t1, t2, t3, i0, i1, i2, i3, gh, ghr, gs, gr,
    back_s, back_r, rs_a, rs_b, rs_c, rs_d, ag_a, ag_b, ag_c, as_, ar, local,
):
    place = Place(rows, cols)
    c = place.c
    tokens, full = x1_full.shape
    width = full // cols
    place.greet(rows=True, cols=True, partner=True)

    def token_cols(ref):
        return lambda block: ref.at[:, pl.ds(pl.multiple_of(block * tokens, tokens), tokens)]

    returning = RowExchange(
        place, token_cols(back), lambda source: inbox.at[source], back_s, back_r, local.at[0]
    )
    returning.start()
    grads = GradExchange(
        place, 1, (m0, m1, m2, m3), (t0, t1, t2, t3), (i0, i1, i2, i3), gh, ghr, gs, gr
    )
    own = pl.ds(pl.multiple_of(c * width, width), width)
    small[...] = jnp.zeros_like(small)
    small[11:12, :] = jnp.sum(cot_full[:, own].astype(F32), axis=0, keepdims=True)
    unit_sums(d_hidden, small, width)
    across_tokens(hidden, cot_full, m3)
    grads.hand(3)
    returning.arrive()
    for head in range(rows):
        attn_t[head * HEAD_DIM : (head + 1) * HEAD_DIM, :] = inbox[head, :HEAD_DIM, :]
    d_projection(inbox, HEAD_DIM, cos, sin, rows, d_pre, small)
    d_norms(
        x1_full, d_pre, wq1, d_normed, vec_all[1, 0:1, :], vec_all[1, 1:2, :], total, low, sums
    )

    def produce(summed, mine):
        unit, rstd = unit_rows(x1_full[mine, :].astype(F32))
        moved = (
            summed
            - jnp.mean(summed, axis=1, keepdims=True)
            - unit * jnp.mean(summed * unit, axis=1, keepdims=True)
        )
        return (cot_full[mine, :].astype(F32) + rstd * moved).astype(BF)

    def work(time):
        if time == 0:
            across_tokens(normed_m, d_hidden, m1)
            grads.hand(1)
        if time == 1:
            grads.merge(3)
            across_tokens(normed_a, d_pre, m0, at=0)
            grads.hand(0)
        if time == 2:
            for at in range(0, full, 256):
                m2[:, at : at + 256] = dot(attn_t[...], cot_full[:, at : at + 256]).astype(BF)
            grads.hand(2)
        if time == 3:
            grads.merge(1)
        if time == 4:
            grads.merge(0)
            grads.merge(2)

    line_sum(
        place, total, low, from_left, from_right, grad_full, (rs_a, rs_b, rs_c, rs_d),
        (ag_a, ag_b, ag_c), PARTS, produce, work,
    )
    flipped = dot(grad_full[...], wo0[...], ((1,), (1,))).T
    for head in range(rows):
        pieces[head] = flipped[head * HEAD_DIM : (head + 1) * HEAD_DIM].astype(BF)
    exchange = RowExchange(
        place, lambda target: pieces.at[target], token_cols(d_out), as_, ar, local.at[1]
    )
    exchange.start()

    def times_slope(value, where):
        return (value * slope0[:, where]).astype(BF)

    times_tiles(grad_full, wp0, d_hidden0, times_slope, ((1,), (1,)))
    times_tiles(d_hidden0, wf0, d_normed0, None, ((1,), (1,)))
    exchange.arrive()
    exchange.finish()
    returning.finish()
    for kind, out in ((3, gw_p), (1, gw_f), (0, gw_q), (2, gw_o)):
        grads.take(kind, out)
    for kind in range(4):
        grads.finish(kind)


def turning(
    rows, cols, back, x1_full, cot_full, vec_all, wq1, wo0, wp0, wf0, normed_a, normed_m, hidden, d_hidden, d_normed, slope0, cos, sin
):
    tokens, full = x1_full.shape
    width, units = full // cols, wf0.shape[1]
    grad_refs, grad_outs = grad_scratch(rows, full, width, units)
    outs = [
        ((width, tokens), BF),
        ((tokens, full), BF),
        ((HEAD_DIM, rows * tokens), BF),
        ((tokens, units), BF),
        ((tokens, full), F32),
        ((8, full), F32),
        ((16, width), F32),
    ] + grad_outs
    scratch = (
        [
            pltpu.VMEM((rows, 4 * HEAD_DIM, tokens), BF),
            pltpu.VMEM((tokens, 3 * width), BF),
            pltpu.VMEM((tokens, full), F32),
            pltpu.VMEM((tokens, full), BF),
            pltpu.VMEM((tokens, full), BF),
            pltpu.VMEM((tokens, full), BF),
            pltpu.VMEM((rows, HEAD_DIM, tokens), BF),
        ]
        + grad_refs
        + [dma(rows)] * 2
        + [dma(PARTS, cols)] * 7
        + [dma(rows)] * 2
        + [dma(2)]
    )
    return kernel_call(
        partial(turning_kernel, rows, cols), 3, outs, scratch,
        back, x1_full, cot_full, vec_all, wq1, wo0, wp0, wf0, normed_a, normed_m, hidden, d_hidden, d_normed, slope0, cos, sin,
    )


def closing_kernel(
    rows, cols,
    back, x_full, x1_full, grad_full, vec_all, wq0, wo1, attn_t0, attn_t1, normed_a, normed_m, hidden, d_hidden, d_normed, branch1, sums1, small1, g1_q, g1_f, g1_o, g1_p, cos, sin,
    out_rows, grad_rows, small_out, gw_q, gw_f, gw_o, gw_p,
    inbox, d_pre, total, low, from_left, from_right, o_total, o_low, o_left, o_right, sums, small, line_sums, line_in, col_in, row_in, o_own, g_own,
    m0, m1, m2, m3, t0, t1, t2, t3, i0, i1, i2, i3, gh, ghr, gs, gr,
    back_s, back_r, rs_a, rs_b, rs_c, rs_d, os_a, os_b, os_c, os_d, ls_s, ls_r, cs_s, cs_r, rw_s, rw_r, sw_s, sw_r, local,
):
    place = Place(rows, cols)
    s, r, c = place.s, place.r, place.c
    tokens, full = x_full.shape
    width = full // cols
    place.greet(rows=True, cols=True, partner=True, cross_rows=True)
    own = pl.ds(pl.multiple_of(c * width, width), width)

    def features(owner):
        return (slice(None), pl.ds(pl.multiple_of(owner * width, width), width))

    returning = RowExchange(
        place,
        lambda target: back.at[:, pl.ds(pl.multiple_of(target * tokens, tokens), tokens)],
        lambda source: inbox.at[source],
        back_s, back_r, local.at[0],
    )
    returning.start()
    attn_rows = attn_t1[...].astype(F32).T.astype(BF)
    tile = min(256, full)
    for at in range(0, full, tile):
        value = branch1[:, at : at + tile] + dot(attn_rows, wo1[:, at : at + tile])
        o_total[:, at : at + tile] = value
        o_low[:, at : at + tile] = value.astype(BF)
    out_sum = LineReduce(
        place, o_total, o_low, o_left, o_right, features, (os_a, os_b, os_c, os_d)
    )
    grad_sum = LineReduce(
        place, total, low, from_left, from_right, features, (rs_a, rs_b, rs_c, rs_d)
    )
    grads = GradExchange(
        place, 0, (m0, m1, m2, m3), (t0, t1, t2, t3), (i0, i1, i2, i3), gh, ghr, gs, gr
    )
    out_sum.step(0)
    across_tokens(hidden, grad_full, m3)
    grads.hand(3)
    small[...] = jnp.zeros_like(small)
    small[1] = small1[...]
    small[0, 11:12, :] = jnp.sum(grad_full[:, own].astype(F32), axis=0, keepdims=True)
    unit_sums(d_hidden, small.at[0], width)
    returning.arrive()
    d_projection(inbox, 0, cos, sin, rows, d_pre, small.at[0])
    lane = lax.broadcasted_iota(jnp.int32, (min(128, tokens), 128), 1)

    def row_sums(where, joined, unit):
        first = jnp.sum(joined, axis=1, keepdims=True)
        second = jnp.sum(joined * unit, axis=1, keepdims=True)
        both = jnp.where(lane == 0, first, jnp.where(lane == 1, second, 0.0))
        line_sums[:, where] = both.T[:8]

    d_norms(
        x_full, d_pre, wq0, d_normed, vec_all[0, 0:1, :], vec_all[0, 1:2, :], total, low,
        sums.at[0], row_sums,
    )
    sums[1] = sums1[...]

    def line_copy(step):
        return rcopy(
            line_sums, line_in.at[step], ls_s.at[step], ls_r.at[step], col=place.col_to(step)
        )

    def col_copy(step):
        target = place.col_to(step)
        piece = sums.at[:, :, pl.ds(pl.multiple_of(target * width, width), width)]
        return rcopy(piece, col_in.at[step], cs_s.at[step], cs_r.at[step], col=target)

    def row_copy(ds, step):
        index = ds * rows + step
        layer = lax.rem(s + ds, 2)
        return rcopy(
            small.at[layer], row_in.at[index], rw_s.at[index], rw_r.at[index],
            section=layer, row=place.row_to(step),
        )

    for step in range(1, cols):
        line_copy(step).start()
        col_copy(step).start()
    grad_sum.step(0)
    out_sum.step(1)
    across_tokens(normed_m, d_hidden, m1)
    grads.hand(1)
    grads.merge(3)
    across_tokens(normed_a, d_pre, m0, at=0)
    grads.hand(0)
    out_sum.step(2)
    grad_sum.step(1)
    for at in range(0, full, tile):
        m2[:, at : at + tile] = dot(attn_t0[...], grad_full[:, at : at + tile]).astype(BF)
    grads.hand(2)
    grads.merge(1)
    for step in range(1, cols):
        col_copy(step).wait_recv()
    head = sums[:, :, own]
    for step in range(1, cols):
        head = head + col_in[step]
    small[:, :8, :] = head
    others = [(ds, step) for ds in range(2) for step in range(rows) if ds or step]
    for ds, step in others:
        row_copy(ds, step).start()
    out_own = x1_full[:, own].astype(F32) + out_sum.own() + vec_all[1, 7:8, own]
    o_own[1] = out_own.astype(BF)
    o_own[0] = x1_full[:, own]
    grads.merge(0)
    grads.merge(2)

    def swap_copy(index, source, target):
        return rcopy(
            source.at[1 - s], target.at[s], sw_s.at[index], sw_r.at[index], section=1 - s
        )

    out_swap = swap_copy(0, o_own, out_rows)
    grad_swap = swap_copy(1, g_own, grad_rows)
    out_swap.start()
    out_keep = pltpu.make_async_copy(o_own.at[s], out_rows.at[s], local.at[1])
    out_keep.start()
    grad_sum.step(2)
    joined = line_sums[...]
    for step in range(1, cols):
        line_copy(step).wait_recv()
        joined = joined + line_in[step]
    wide = jnp.concatenate([joined, jnp.zeros((120, tokens), F32)], axis=0).T
    unit, rstd = unit_rows(x_full[...].astype(F32))
    o_total[...] = unit
    moved = (
        grad_sum.own() - wide[:, 0:1] / full - o_total[:, own] * (wide[:, 1:2] / full)
    )
    g_own[0] = (grad_full[:, own].astype(F32) + rstd * moved).astype(BF)
    g_own[1] = grad_full[:, own]
    grad_swap.start()
    grad_keep = pltpu.make_async_copy(g_own.at[s], grad_rows.at[s], local.at[2])
    grad_keep.start()
    mine = small[s]
    for ds, step in others:
        row_copy(ds, step).wait_recv()
        mine = mine + row_in[ds * rows + step]
    small_out[...] = mine
    for kind, out, later in ((3, gw_p, g1_p), (1, gw_f, g1_f), (0, gw_q, g1_q), (2, gw_o, g1_o)):

        @pl.when(s == 1)
        def _():
            out[...] = later[...]

        grads.take(kind, out)
    out_keep.wait()
    grad_keep.wait()
    out_swap.wait()
    grad_swap.wait()
    returning.finish()
    out_sum.finish()
    grad_sum.finish()
    for step in range(1, cols):
        line_copy(step).wait_send()
        col_copy(step).wait_send()
    for ds, step in others:
        row_copy(ds, step).wait_send()
    for kind in range(4):
        grads.finish(kind)


def closing(
    rows, cols, back, x_full, x1_full, grad_full, vec_all, wq0, wo1, attn_t0, attn_t1, normed_a, normed_m, hidden, d_hidden, d_normed, branch1, sums1, small1, later, cos, sin
):
    tokens, full = x_full.shape
    width, units = full // cols, hidden.shape[1]
    grad_refs, grad_outs = grad_scratch(rows, full, width, units)
    outs = [
        ((2, tokens, width), BF),
        ((2, tokens, width), BF),
        ((16, width), F32),
    ] + grad_outs
    wide = [
        pltpu.VMEM((tokens, full), F32),
        pltpu.VMEM((tokens, full), BF),
        pltpu.VMEM((tokens, full), BF),
        pltpu.VMEM((tokens, full), BF),
    ]
    scratch = (
        [pltpu.VMEM((rows, 3 * HEAD_DIM, tokens), BF), pltpu.VMEM((tokens, 3 * width), BF)]
        + wide
        + wide
        + [
            pltpu.VMEM((2, 8, full), F32),
            pltpu.VMEM((2, 16, width), F32),
            pltpu.VMEM((8, tokens), F32),
            pltpu.VMEM((cols, 8, tokens), F32),
            pltpu.VMEM((cols, 2, 8, width), F32),
            pltpu.VMEM((2 * rows, 16, width), F32),
            pltpu.VMEM((2, tokens, width), BF),
            pltpu.VMEM((2, tokens, width), BF),
        ]
        + grad_refs
        + [dma(rows)] * 2
        + [dma(1, cols)] * 8
        + [dma(cols)] * 4
        + [dma(2 * rows)] * 2
        + [dma(2)] * 2
        + [dma(3)]
    )
    return kernel_call(
        partial(closing_kernel, rows, cols), 4, outs, scratch,
        back, x_full, x1_full, grad_full, vec_all, wq0, wo1, attn_t0, attn_t1, normed_a, normed_m, hidden, d_hidden, d_normed, branch1, sums1, small1, *later, cos, sin,
    )


def relay_body(
    hidden_in,
    cotangent,
    lengths,
    norm_gains,
    norm_biases,
    w_qkv,
    b_qkv,
    w_out,
    w_fc,
    b_fc,
    w_proj,
    b_out,
):
    rows, cols = lax.axis_size("row"), lax.axis_size("col")
    tokens, width = hidden_in.shape[1:]
    section = lax.axis_index("section")
    lengths_row = lax.dynamic_index_in_dim(lengths, section, 0, keepdims=False)
    all_tokens = jnp.arange(tokens * rows, dtype=jnp.int32)
    my_tokens = lax.axis_index("row") * tokens + jnp.arange(tokens, dtype=jnp.int32)
    starts, segment, position = token_layout(lengths_row, my_tokens)
    cos, sin = rotary_tables(position, ROT)
    cos, sin = cos.T, sin.T
    segments = segment_of(all_tokens, starts)
    labels = jnp.arange(1, lengths_row.shape[0], dtype=jnp.int32)
    first = jnp.sum(
        jnp.where(segments[:, None] == labels[None, :], starts[None, 1:], 0), axis=1
    )[None]
    prompt = lengths_row[:1]
    vectors = jnp.concatenate(
        [norm_gains[0], norm_biases[0], b_qkv[0], b_out, b_fc[0].reshape(-1, width)], axis=0
    )
    vectors = jnp.pad(vectors, ((0, 16 - vectors.shape[0]), (0, 0)))
    blocks = (w_qkv[0], w_fc[0], w_out[0], w_proj[0])
    (
        x_full, cot_full, vec_all, wq0, wf0, wo0, wp0, normed_a0, normed_m0, qkv0, hidden0, slope0, branch0,
    ) = opening(rows, cols, hidden_in, cotangent, vectors, *blocks, cos, sin)
    out0, low0, log0 = attention_forward(prompt, first, qkv0)
    (
        attn_t0, x1_full, wq1, wf1, wo1, wp1, normed_a1, normed_m1, qkvd1, hidden1, d_hidden1, branch1, d_normed1,
    ) = middle(
        rows, cols, low0, wo0, branch0, x_full, vec_all, *blocks, cot_full, cos, sin
    )
    back1 = attention_both(prompt, first, qkvd1)
    attn_t1, grad_full, d_out0, d_hidden0, d_normed0, sums1, small1, *later = turning(
        rows, cols, back1, x1_full, cot_full, vec_all, wq1, wo0, wp0, wf0, normed_a1, normed_m1,
        hidden1, d_hidden1, d_normed1, slope0, cos, sin,
    )
    back0 = attention_backward(prompt, first, qkv0, d_out0, out0, log0)
    out_rows, grad_rows, small, gw_q, gw_f, gw_o, gw_p = closing(
        rows, cols, back0, x_full, x1_full, grad_full, vec_all, wq0, wo1, attn_t0, attn_t1,
        normed_a0, normed_m0, hidden0, d_hidden0, d_normed0, branch1, sums1, small1, later, cos, sin,
    )
    return (
        out_rows[None],
        grad_rows[None],
        small[None, 0:2],
        small[None, 2:4],
        gw_q[None],
        small[None, 8:11],
        gw_o[None],
        gw_f[None],
        small[12 : 12 + b_fc.shape[1] // width].reshape(1, -1),
        gw_p[None],
        small[11:12],
    )


def fits(mesh):
    rows, cols = mesh.shape["row"], mesh.shape["col"]
    return rows == cols and MODEL_WIDTH == rows * cols * HEAD_DIM


def solution(mesh):
    return jax.shard_map(
        relay_body if fits(mesh) else body,
        mesh=mesh,
        in_specs=(
            P(None, "row", "col"),
            P(None, "row", "col"),
            P(),
            P("section", None, "col"),
            P("section", None, "col"),
            P("section", None, "row", "col"),
            P("section", None, "col"),
            P("section", "col", "row"),
            P("section", "row", "col"),
            P("section", "col"),
            P("section", "col", "row"),
            P("section", "col"),
        ),
        out_specs=(
            P("section", None, "row", "col"),
            P("section", None, "row", "col"),
            P("section", None, "col"),
            P("section", None, "col"),
            P("section", None, "row", "col"),
            P("section", None, "col"),
            P("section", "col", "row"),
            P("section", "row", "col"),
            P("section", "col"),
            P("section", "col", "row"),
            P("section", "col"),
        ),
        check_vma=False,
    )
```

time: 1440 us -> 359 us (0.25)
  waiting for transfers between devices: 701 us -> 0 us
  matrix products: 370 us -> 0 us
  Pallas kernels: 0 us -> 336 us
  other arithmetic: 137 us -> 3.98 us
  blocking collectives: 94.6 us -> 0 us
  local copies, waits for them, and re-layouts: 105 us -> 16.7 us
  between operations: 19.1 us -> 0.75 us
    dot_general x134 -> x0, matrix products: 370 us -> none  [the longest x16 47.4 us: body(): jnp.einsum('qhd,khd->hqk', grad_out3, value_part, preferred_element_type=...]
    all_gather x22 -> x0, waiting for transfers between devices: 357 us -> none  [the longest x4 78.2 us: body(): lax.all_gather(key_flat, 'row', axis=0, tiled=True)]
    reduce_scatter x19 -> x0, waiting for transfers between devices: 338 us -> none  [the longest x4 113 us: body(): lax.psum_scatter(grad_normed_a.astype(jnp.bfloat16), 'col', scatter_dimen...]
    pallas_call x0 -> x7, Pallas kernels: none -> 336 us  [the longest x4 268 us: kernel_call(): pl.pallas_call(kernel, out_shape=[jax.ShapeDtypeStruct(shape, dtype) for...]
    psum x5 -> x0, blocking collectives: 54.3 us -> none  [the longest x4 37.6 us: body(): lax.psum(jnp.stack([jnp.sum(gradient_unit_rows, axis=1), jnp.sum(gradient...]
    reduce_sum x25 -> x2, other arithmetic: 46.4 us -> 0.78 us  [the longest x1 0.69 us: relay_body(): jnp.sum(jnp.where(segments[:, None] == labels[None, :], starts[None, 1:],...]
    all_gather x3 -> x0, blocking collectives: 40.3 us -> none  [the longest x1 14.7 us: body(): lax.all_gather(w_out[0], 'row', axis=1, tiled=True)]
    concatenate x16 -> x0, other arithmetic: 33.9 us -> none  [the longest x4 27.5 us: body(): jnp.concatenate([jnp.concatenate(key_terms, axis=0), jnp.concatenate(valu...]
  transfers between devices with their start and end apart: 44 -> 0, of which waited for: 38 -> 0; matrix products, arithmetic and copies ran while one was open for 29% -> 0% of each run, Pallas kernels for 0% -> 0%
where the time goes in v1:
time: 359 us; the launch traced here: 357 us
  Pallas kernels  336 us (94%)
  local copies, waits for them, and re-layouts  16.7 us (5%)
  other arithmetic  3.98 us (1%)
    pallas_call x4, Pallas kernels, kernel_call(): pl.pallas_call(kernel, out_shape=[jax.ShapeDtypeStruct(shape, dtype) for...  268 us
    pallas_call x3, Pallas kernels, attention_call(): pl.pallas_call(partial(kernel, min(ATTENTION_BLOCK, total)), out_shape=[j...  68 us
    unnamed x21, local copies, waits for them, and re-layouts  10.4 us

profile of v1, /device:TPU:0, one launch (start us, length us, event | category | flops | bytes accessed | tf_op | source)
XLA Modules:
  0.0 357.4 jit_solution(4850841504547183629)
XLA Ops:
  0.7 0.7 fusion.4
  1.3 0.2 reduce-window.9
  1.5 0.7 bitcast_subtract_fusion
  2.3 0.7 constant_dynamic-slice_fusion
  3.1 0.1 fusion.3
  3.2 0.5 broadcast.64
  3.7 1.3 reduce.3
  5.1 0.7 copy.28
  5.8 0.7 concatenate.3
  6.5 0.6 pad.4.vectors
  7.1 0.1 fusion
  7.2 0.7 fusion.1
  7.9 0.8 multiply_sine_fusion
  8.7 64.2 %shard_map.203 = (bf16[512,1024]{1,0:T(8,128)(2,1)}, bf16[512,1024]{1,0:T(8,128)(2,1)}, f32[2,16,1024]{2,1,0:T(8,128)}, bf16[3,1024,256]{2,1,0:T(8,128)(2,1)}, b...) custom-call(bf16[2,512,256]{2,1,0:T(8,128)(2,1)} %hidden_in.1, ...), custom_call_target="tpu_custom_call" | custom-call | tf_op jit(solution)/shard_map/pallas_call | solution.py:819
  72.8 17.1 %shard_map.204 = (f32[64,2048]{1,0:T(8,128)}, bf16[64,2048]{1,0:T(8,128)(2,1)}, f32[1,2048]{1,0:T(1,128)}) custom-call(s32[1]{0:T(128)} %bitcast.54, s32[1,2048]{1,0:T(1,128)} %bitcast.49, bf16[192,2048]{1,0:T(8,128)(2,1)} %get-tuple-element.56.qkv), custom_call_target="tpu_custom_call" | custom-call | tf_op jit(solution)/shard_map/pallas_call | solution.py:984
  89.9 66.3 %shard_map.205 = (bf16[256,512]{1,0:T(8,128)(2,1)}, bf16[512,1024]{1,0:T(8,128)(2,1)}, bf16[3,1024,256]{2,1,0:T(8,128)(2,1)}, bf16[1024,1024]{1,0:T(8,128)(2,1)}...) custom-call(bf16[64,2048]{1,0:T(8,128)(2,1)} %get-tuple-element.57.a, ...), custom_call_target="tpu_custom_call" | custom-call | tf_op jit(solution)/shard_map/pallas_call | solution.py:819
  156.2 32.6 %shard_map.206.back = bf16[256,2048]{1,0:T(8,128)(2,1)} custom-call(s32[1]{0:T(128)} %bitcast.55, s32[1,2048]{1,0:T(1,128)} %bitcast.50, bf16[256,2048]{1,0:T(8,128)(2,1)} %get-tuple-element.63.qkvd), custom_call_target="tpu_custom_call" | custom-call | tf_op jit(solution)/shard_map/pallas_call | solution.py:984
  188.8 70.5 %shard_map.207 = (bf16[256,512]{1,0:T(8,128)(2,1)}, bf16[512,1024]{1,0:T(8,128)(2,1)}, bf16[64,2048]{1,0:T(8,128)(2,1)}, bf16[512,1024]{1,0:T(8,128)(2,1)}, f32[...) custom-call(bf16[256,2048]{1,0:T(8,128)(2,1)} %shard_map.206.back, ...), custom_call_target="tpu_custom_call" | custom-call | tf_op jit(solution)/shard_map/pallas_call | solution.py:819
  259.4 18.3 %shard_map.208.back = bf16[192,2048]{1,0:T(8,128)(2,1)} custom-call(s32[1]{0:T(128)} %bitcast.56, s32[1,2048]{1,0:T(1,128)} %bitcast.51, bf16[192,2048]{1,0:T(8,128)(2,1)} %get-tuple-element.56.qkv, bf16[64,2048]{1,0:T(8,128)(2,1)} %get-tuple-element.74.d_out, f32[64,2048]{1,0:T(8,128)} %get-tuple-element.75.out, f32[1,2048]{1,0:T(1,128)} %get-tuple-element.76.log_sum), custom_call_target="tpu_custom_call" | custom-call | tf_op jit(solution)/shard_map/pallas_call | solution.py:984
  277.7 67.0 %shard_map.209 = (bf16[2,512,256]{2,1,0:T(8,128)(2,1)}, bf16[2,512,256]{2,1,0:T(8,128)(2,1)}, f32[16,256]{1,0:T(8,128)}, f32[3,256,256]{2,1,0:T(8,128)}, f32[256...) custom-call(bf16[192,2048]{1,0:T(8,128)(2,1)} %shard_map.208.back, ...), custom_call_target="tpu_custom_call" | custom-call | tf_op jit(solution)/shard_map/pallas_call | solution.py:819
  344.8 1.3 slice.35
  346.1 0.7 slice_bitcast_fusion
  346.8 0.6 copy.26
  347.4 0.7 slice_bitcast_fusion.1
  348.1 1.4 slice_bitcast_fusion.2
  349.5 0.6 copy.24
  350.0 2.0 copy.35
  352.0 1.9 copy.36
  353.9 0.9 copy.37
  354.8 0.7 copy.38
  355.5 1.0 copy.39
  356.4 1.0 copy.40
  (17 shorter events, 0.2 us)
Async XLA Ops:
  3.0 69.9 %copy-start.4 = (s32[1,3]{1,0:T(1,128)}, s32[1,3]{1,0:T(1,128)S(1)}, u32[]{:S(2)}) copy-start(s32[1,3]{1,0:T(1,128)S(1)} %constant_dynamic-slice_fusion) | copy-start | bytes 40
  344.7 9.1 %copy-start.2 = (f32[3,256,256]{2,1,0:T(8,128)S(1)}, f32[3,256,256]{2,1,0:T(8,128)}, u32[]{:S(2)}) copy-start(f32[3,256,256]{2,1,0:T(8,128)} %get-tuple-element.97) | copy-start | bytes 2359300
  344.8 10.0 %copy-start.3 = (f32[256,256]{1,0:T(8,128)S(1)}, f32[256,256]{1,0:T(8,128)}, u32[]{:S(2)}) copy-start(f32[256,256]{1,0:T(8,128)} %get-tuple-element.98) | copy-start | bytes 786436
  350.0 5.4 %copy-start.1 = (f32[256,1024]{1,0:T(8,128)S(1)}, f32[256,1024]{1,0:T(8,128)}, u32[]{:S(2)}) copy-start(f32[256,1024]{1,0:T(8,128)} %get-tuple-element.99) | copy-start | bytes 3145732
  353.9 2.6 copy-start
